TPU v7x, 32 devices: a whole 2x2x4 slice. The times are simulated.
32 devices in a mesh: batch: 8 (over y, x, core), height: 4 (over z).
Axes of the slice: x: 2, y: 2, z: 4, core: 2. Of those that a mesh axis runs over, the one named last changes fastest.
Arguments:
- images: bfloat16 [192, 32, 32, 1024], P('batch', 'height'), may hold values from -8 to 8
- w_first: bfloat16 [1024, 1024], replicated, may hold values from -0.1875 to 0.1875
- gain_first: float32 [1024], replicated, may hold values from 0.25 to 1.75
- shift_first: float32 [1024], replicated, may hold values from -3 to 3
- w_mid: bfloat16 [3, 3, 32, 1024], replicated, may hold values from -0.375 to 0.375
- gain_mid: float32 [1024], replicated, may hold values from 0.25 to 1.75
- shift_mid: float32 [1024], replicated, may hold values from -3 to 3
- w_last: bfloat16 [1024, 2048], replicated, may hold values from -0.1875 to 0.1875
- gain_last: float32 [2048], replicated, may hold values from 0.25 to 1.75
- shift_last: float32 [2048], replicated, may hold values from -3 to 3
- w_side: bfloat16 [1024, 2048], replicated, may hold values from -0.1875 to 0.1875
- gain_side: float32 [2048], replicated, may hold values from 0.25 to 1.75
- shift_side: float32 [2048], replicated, may hold values from -3 to 3
- cotangent: bfloat16 [192, 16, 16, 2048], P('batch', 'height'), may hold values from -6 to 6
Outputs:
- output: bfloat16 [192, 16, 16, 2048], P('batch', 'height')
- grad_images: bfloat16 [192, 32, 32, 1024], P('batch', 'height')
- grad_first: float32 [1024, 1024], replicated
- grad_gain_first: float32 [1024], replicated
- grad_shift_first: float32 [1024], replicated
- grad_mid: float32 [3, 3, 32, 1024], replicated
- grad_gain_mid: float32 [1024], replicated
- grad_shift_mid: float32 [1024], replicated
- grad_last: float32 [1024, 2048], replicated
- grad_gain_last: float32 [2048], replicated
- grad_shift_last: float32 [2048], replicated
- grad_side: float32 [1024, 2048], replicated
- grad_gain_side: float32 [2048], replicated
- grad_shift_side: float32 [2048], replicated
All inputs are finite; a program needn't handle non-finite values.
Results may differ from a plain program's by a relative error of at most 0.0084.
Values may be sent and summed in bfloat16 or wider, within the bound.
A program may use at most 704 MiB of HBM per device.

v0:
```python
import functools

import jax
import jax.numpy as jnp
from jax import lax
from jax.experimental import pallas as pl
from jax.experimental.pallas import tpu as pltpu
from jax.sharding import PartitionSpec as P

EPSILON = 1e-05
LANES = 128
CHUNK = 256
BF16 = jnp.bfloat16
F32 = jnp.float32
MIB = 1 << 20


def dot(a, b):
    return jnp.dot(a, b, preferred_element_type=F32)


def dot_nt(a, b):
    return lax.dot_general(a, b, (((1,), (1,)), ((), ())), preferred_element_type=F32)


def dot_tn(a, b):
    return lax.dot_general(a, b, (((0,), (0,)), ((), ())), preferred_element_type=F32)


def fold(values):
    rows, cols = values.shape
    return jnp.sum(values.reshape(rows // 8, 8, cols), axis=0)


def put_row(ref, first, row):
    for k in range(row.shape[1] // LANES):
        ref[first + k : first + k + 1, :] = row[:, k * LANES : (k + 1) * LANES]


def get_row(values, first, width):
    count = width // LANES
    return jnp.concatenate([values[first + k : first + k + 1, :] for k in range(count)], axis=1)


def sums_out(ref, *partials):
    first = 0
    for part in partials:
        row = jnp.sum(part, axis=0, keepdims=True)
        put_row(ref, first, row)
        first += row.shape[1] // LANES


def whole(shape):
    return pl.BlockSpec(shape, lambda *_: (0,) * len(shape), pipeline_mode=pl.Buffered(1))


def rows_spec(rows, cols):
    return pl.BlockSpec((rows, cols), lambda i: (i, 0))


def call(
    body, name, grid, in_specs, out_specs, out_shape, scratch=(), flops=0, moved=0, vmem=56, ident=None
):
    return pl.pallas_call(
        body,
        name=name,
        grid=grid,
        in_specs=in_specs,
        out_specs=out_specs,
        out_shape=out_shape,
        scratch_shapes=list(scratch),
        compiler_params=pltpu.CompilerParams(
            vmem_limit_bytes=vmem * MIB, collective_id=ident, has_side_effects=ident is not None
        ),
        cost_estimate=pl.CostEstimate(flops=flops, bytes_accessed=moved, transcendentals=0),
    )


def shape(dims, kind=F32):
    return jax.ShapeDtypeStruct(dims, kind)


def everyone():
    batch, height = lax.axis_index("batch"), lax.axis_index("height")
    size_b, size_h = lax.axis_size("batch"), lax.axis_size("height")
    row = [(lax.rem(batch + k, size_b), height) for k in range(1, size_b)]
    return row, [(batch, lax.rem(height + k, size_h)) for k in range(1, size_h)]


def signal(peers):
    barrier = pltpu.get_barrier_semaphore()
    for one in peers:
        pl.semaphore_signal(barrier, inc=1, device_id=one, device_id_type=pl.DeviceIdType.MESH)


def signal_all():
    row, column = everyone()
    signal(row + column)


def wait_all():
    row, column = everyone()
    pl.semaphore_wait(pltpu.get_barrier_semaphore(), len(row + column))


def wait_partners():
    pl.semaphore_wait(pltpu.get_barrier_semaphore(), len(partners()))


def greet(peers):
    signal(peers)
    pl.semaphore_wait(pltpu.get_barrier_semaphore(), len(peers))


def exchange_scratch(rows):
    size_b, size_h = lax.axis_size("batch"), lax.axis_size("height")
    dma = pltpu.SemaphoreType.DMA
    return [
        pltpu.VMEM((rows, LANES), F32),
        pltpu.VMEM((size_b, rows, LANES), F32),
        pltpu.VMEM((size_h, rows, LANES), F32),
        dma((size_b - 1,)),
        dma((size_b,)),
        dma((size_h - 1,)),
        dma((size_h,)),
    ]


class Exchange:
    def __init__(self, scratch):
        self.stat, self.got_b, self.got_h, self.send_b, self.recv_b, self.send_h, self.recv_h = scratch
        self.me_b, self.me_h = lax.axis_index("batch"), lax.axis_index("height")
        self.row, self.column = everyone()

    def spread(self, src, got, me, targets, send, recv):
        return [
            remote(src, got.at[me], send.at[k], recv.at[me], target) for k, target in enumerate(targets)
        ]

    def total(self, src, got, me, targets, send, recv):
        size = got.shape[0]
        for k, target in enumerate(targets):
            other = lax.rem(me + (size - 1 - k), size)
            remote(src, got.at[other], send.at[k], recv.at[other], target).wait_recv()
        total = got[0]
        for k in range(1, size):
            total = total + got[k]
        return total

    def over_batch(self):
        return self.stat, self.got_b, self.me_b, self.row, self.send_b, self.recv_b

    def over_height(self):
        return self.got_h.at[self.me_h], self.got_h, self.me_h, self.column, self.send_h, self.recv_h

    def start(self):
        run(self.spread(*self.over_batch()), "start")
        self.got_b[self.me_b] = self.stat[...]

    def turn(self):
        self.got_h[self.me_h] = self.total(*self.over_batch())
        run(self.spread(*self.over_height()), "start")

    def finish(self, epilogue, params, outs):
        epilogue(self.total(*self.over_height()), params, outs)
        run(self.spread(*self.over_batch()) + self.spread(*self.over_height()), "wait_send")


def exchange(scratch, epilogue, params, outs):
    one = Exchange(scratch)
    one.start()
    one.turn()
    one.finish(epilogue, params, outs)


def norm_terms(total, first, width, cells):
    average = get_row(total, first, width) * (1.0 / cells)
    meansq = get_row(total, first + width // LANES, width) * (1.0 / cells)
    inverse = lax.rsqrt(meansq - average * average + EPSILON)
    return inverse, -average * inverse


def fill(ref, rows):
    for k, row in enumerate(rows):
        ref[k : k + 1, :] = row
    ref[len(rows) :, :] = jnp.zeros((8 - len(rows), ref.shape[1]), F32)


def act_rows(inverse, offset, gain, shift):
    return [
        inverse,
        offset,
        0.5 * gain,
        0.5 * shift,
        0.5 * gain * inverse,
        0.5 * (shift + gain * offset),
    ]


def first_totals(cells_in, cells_out, width, wide, total, params, outs):
    gain, shift = as_row(params[0]), as_row(params[1])
    fill(outs[0], act_rows(*norm_terms(total, 0, width, cells_in), gain, shift))
    fill(outs[1], list(norm_terms(total, 2 * width // LANES, wide, cells_out)))


def mid_totals(cells_out, width, total, params, outs):
    gain, shift = as_row(params[0]), as_row(params[1])
    fill(outs[0], act_rows(*norm_terms(total, 0, width, cells_out), gain, shift))


def last_totals(cells_out, wide, total, params, outs):
    gain_last, shift_last, gain_side, shift_side, side = params
    inverse, offset = norm_terms(total, 0, wide, cells_out)
    inverse_s, offset_s = side[0:1, :], side[1:2, :]
    gain_l, gain_s = 0.5 * as_row(gain_last), 0.5 * as_row(gain_side)
    shift = 0.5 * (as_row(shift_last) + as_row(shift_side))
    scales = [gain_l * inverse, gain_s * inverse_s, gain_l * offset + gain_s * offset_s + shift]
    fill(outs[0], [inverse, offset, inverse_s, offset_s] + scales)


def back_rows(scale, total_up, cross, cells):
    return [0.5 * scale, -scale * total_up * (1.0 / cells), -scale * cross * (1.0 / cells)]


def folded(rows, inverse, offset):
    scale, base, cross = rows
    return [scale, cross * inverse, base + cross * offset]


def out_totals(cells_out, wide, total, params, outs):
    coef = params[0]
    step = wide // LANES
    total_up, last_raw, side_raw = [0.5 * get_row(total, k * step, wide) for k in range(3)]
    inverse_l, offset_l, inverse_s, offset_s = [coef[k : k + 1, :] for k in range(4)]
    last_cross = inverse_l * last_raw + offset_l * total_up
    side_cross = inverse_s * side_raw + offset_s * total_up
    rows_l = back_rows(2.0 * coef[4:5, :], total_up, last_cross, cells_out)
    rows_s = back_rows(2.0 * coef[5:6, :], total_up, side_cross, cells_out)
    fill(outs[0], folded(rows_l, inverse_l, offset_l) + folded(rows_s, inverse_s, offset_s))
    fill(outs[1], [total_up, last_cross, side_cross])


def inner_totals(cells, width, total, params, outs):
    coef = params[0]
    total_up = 0.5 * get_row(total, 0, width)
    cross = 0.5 * get_row(total, width // LANES, width)
    fill(outs[0], back_rows(2.0 * coef[4:5, :], total_up, cross, cells))
    fill(outs[1], [total_up, cross])


def half_silu(half):
    return half + half * jnp.tanh(half)


def slope_twice(half, th):
    return (1.0 + th) * (1.0 + half * (1.0 - th))


def to_neighbour(copies, moves_up, what):
    height, size = lax.axis_index("height"), lax.axis_size("height")
    sends = height > 0 if moves_up else height < size - 1
    gets = height < size - 1 if moves_up else height > 0
    if what == "start":
        pl.when(sends)(lambda: run(copies, "start"))
    else:
        pl.when(sends)(lambda: run(copies, "wait_send"))
        pl.when(gets)(lambda: run(copies, "wait_recv"))


def planes_matrix(rows, cols, inverse):
    px, q, half = rows * cols, rows * cols // 4, cols // 2
    place = lax.broadcasted_iota(jnp.int32, (px, px), 1 if inverse else 0)
    pixel = lax.broadcasted_iota(jnp.int32, (px, px), 0 if inverse else 1)
    plane, inner = place // q, place % q
    source = (2 * (inner // half) + plane // 2) * cols + 2 * (inner % half) + plane % 2
    return (source == pixel).astype(F32).astype(BF16)


def row_matrix(count, cols):
    size, half = count * cols, cols // 2
    place = lax.broadcasted_iota(jnp.int32, (size, size), 0)
    pixel = lax.broadcasted_iota(jnp.int32, (size, size), 1)
    source = place // cols * cols + 2 * (place % half) + place % cols // half
    return (source == pixel).astype(F32).astype(BF16)


def spread_weights(w, out):
    gw, width = w.shape[1], w.shape[2]
    group = (lax.broadcasted_iota(jnp.int32, (gw, width), 1) % CHUNK) // gw
    for tap in range(9):
        rows = w[tap].astype(F32)
        for g in range(CHUNK // gw):
            out[tap, g * gw : (g + 1) * gw, :] = jnp.where(group == g, rows, 0.0).astype(BF16)


def as_row(ref):
    return ref[...].reshape(1, ref.shape[0])


def first_body(
    per, px, q, totals, img, w1, ws, gain, shift, xp, pre, side, coef, side_coef, acc, acc_s, perm, *ex
):
    step = pl.program_id(0)
    mid, wide = w1.shape[1], ws.shape[1]

    @pl.when(step == 0)
    def _():
        acc[...] = jnp.zeros_like(acc)
        acc_s[...] = jnp.zeros_like(acc_s)
        perm[...] = planes_matrix(img.shape[1], img.shape[2], False)
        signal_all()

    for k in range(per):
        flat = img[k].reshape(px, img.shape[3])
        moved = dot(perm[...], flat).astype(BF16)
        xp[k * px : (k + 1) * px, :] = moved
        for c in range(0, mid, CHUNK):
            cols = slice(c, c + CHUNK)
            part = dot(moved, w1[:, cols])
            pre[k * px : (k + 1) * px, cols] = part
            acc[0:8, cols] += fold(part)
            acc[8:16, cols] += fold(part * part)
    even = jnp.concatenate([xp[k * px : k * px + q, :] for k in range(per)], axis=0)
    for c in range(0, wide, CHUNK):
        cols = slice(c, c + CHUNK)
        part = dot(even, ws[:, cols])
        side[:, cols] = part
        acc_s[0:8, cols] += fold(part)
        acc_s[8:16, cols] += fold(part * part)

    @pl.when(step == pl.num_programs(0) - 1)
    def _():
        sums_out(ex[0], acc[0:8, :], acc[8:16, :], acc_s[0:8, :], acc_s[8:16, :])
        wait_all()
        exchange(ex, totals, [gain, shift], [coef, side_coef])


def conv_body(per, px, q, totals, pre, halo, w1, coef, w, gain, shift, mid, coef2, *scr):
    a00, a01, a10, a11, wbd, perm, acc, *ex = scr
    step = pl.program_id(0)
    width = w1.shape[1]

    @pl.when(step == 0)
    def _():
        acc[...] = jnp.zeros_like(acc)
        spread_weights(w, wbd)
        perm[...] = row_matrix(per, halo.shape[1])
        signal_all()

    scale, offset = coef[4:5, :], coef[5:6, :]
    flat = halo[...].reshape(per * 32, halo.shape[2])
    rim = half_silu(dot(dot(perm[...], flat).astype(BF16), w1[...]) * scale + offset)
    rim = jnp.where(lax.axis_index("height") > 0, rim, 0.0).astype(BF16)
    rim = rim.reshape(per, 2, 16, width)
    a10[:, 0:16, :] = rim[:, 0]
    a11[:, 0:16, :] = rim[:, 1]
    for plane, ref, top in ((0, a00, 0), (1, a01, 0), (2, a10, 16), (3, a11, 16)):
        half = pre[:, plane] * scale[None] + offset[None]
        ref[:, top : top + q, :] = half_silu(half).astype(BF16)
    rows = per * q
    first_col = lax.broadcasted_iota(jnp.int32, (rows, CHUNK), 0) % 16 == 0
    for c in range(0, width, CHUNK):
        cols = slice(c, c + CHUNK)

        def tap(ref, top, row, col):
            return dot(ref[:, top : top + q, cols].reshape(rows, CHUNK), wbd[row * 3 + col, :, cols])

        straight = (
            tap(a00, 0, 1, 1)
            + tap(a01, 0, 1, 2)
            + tap(a10, 16, 2, 1)
            + tap(a11, 16, 2, 2)
            + tap(a10, 0, 0, 1)
            + tap(a11, 0, 0, 2)
        )
        moved = tap(a01, 0, 1, 0) + tap(a11, 16, 2, 0) + tap(a11, 0, 0, 0)
        part = straight + jnp.where(first_col, 0.0, pltpu.roll(moved, 1, 0))
        mid[:, cols] = part
        acc[0:8, cols] += fold(part)
        acc[8:16, cols] += fold(part * part)

    @pl.when(step == pl.num_programs(0) - 1)
    def _():
        sums_out(ex[0], acc[0:8, :], acc[8:16, :])
        wait_all()
        exchange(ex, totals, [gain, shift], [coef2])


def last_body(per, q, totals, mid, coef, w, gl, sl, gs, ss, side_coef, act, pre, coef3, rim, acc, *ex):
    step = pl.program_id(0)
    width = mid.shape[1]

    @pl.when(step == 0)
    def _():
        acc[...] = jnp.zeros_like(acc)
        signal_all()

    top = mid[...].reshape(per, q, width)[:, 0:16] * coef[0:1, :][None] + coef[1:2, :][None]
    rim[...] = top.astype(BF16)
    half = mid[...] * coef[4:5, :] + coef[5:6, :]
    act[...] = half_silu(half).astype(BF16)
    for c in range(0, w.shape[1], CHUNK):
        cols = slice(c, c + CHUNK)
        part = dot(act[...], w[:, cols])
        pre[:, cols] = part
        acc[0:8, cols] += fold(part)
        acc[8:16, cols] += fold(part * part)

    @pl.when(step == pl.num_programs(0) - 1)
    def _():
        sums_out(ex[0], acc[0:8, :], acc[8:16, :])
        wait_all()
        exchange(ex, totals, [gl, sl, gs, ss, side_coef], [coef3])


def rim_copy(rim, halo, per, step, send, recv):
    images = pl.ds(step * per, per)
    return remote(rim.at[images], halo.at[images], send.at[step], recv.at[step], upper_lower()[1])


def rim_finish(rim, halo, per, send, recv):
    copies = [rim_copy(rim, halo, per, s, send, recv) for s in range(rim.shape[0] // per)]
    to_neighbour(copies, True, "wait")


def out_parts(last, side, cot, coef, cols):
    half = last[:, cols] * coef[4:5, cols] + side[:, cols] * coef[5:6, cols] + coef[6:7, cols]
    th = jnp.tanh(half)
    moved = half * th
    up = cot[:, cols].astype(F32) * ((1.0 + th) * (1.0 + (half - moved)))
    return half + moved, up


def out_body(last, side, cot, coef, out, stat, acc):
    step = pl.program_id(0)

    @pl.when(step == 0)
    def _():
        acc[...] = jnp.zeros_like(acc)

    for c in range(0, last.shape[1], CHUNK):
        cols = slice(c, c + CHUNK)
        value, up = out_parts(last, side, cot, coef, cols)
        out[:, cols] = value.astype(BF16)
        acc[0:8, cols] += fold(up)
        acc[8:16, cols] += fold(up * last[:, cols])
        acc[16:24, cols] += fold(up * side[:, cols])

    @pl.when(step == pl.num_programs(0) - 1)
    def _():
        sums_out(stat, acc[0:8, :], acc[8:16, :], acc[16:24, :])


def last_grad_body(totals, last, side, cot, coef, act, stat, rim, lg, sg, g_last, grads, halo, *scr):
    acc, back, send, recv, *ex = scr
    step = pl.program_id(0)
    row = remote(rim, halo, send, recv, upper_lower()[1])

    @pl.when(step == 0)
    def _():
        signal_all()
        acc[...] = jnp.zeros_like(acc)
        ex[0][...] = stat[...]
        wait_all()
        exchange(ex, totals, [coef], [back, grads])
        to_neighbour([row], True, "start")

    for c in range(0, last.shape[1], CHUNK):
        cols = slice(c, c + CHUNK)
        _, part = out_parts(last, side, cot, coef, cols)
        down = part * back[0:1, cols] + last[:, cols] * back[1:2, cols] + back[2:3, cols]
        down = down.astype(BF16)
        lg[:, cols] = down
        acc[:, cols] += dot_tn(act[...], down)
        down = part * back[3:4, cols] + side[:, cols] * back[4:5, cols] + back[5:6, cols]
        sg[:, cols] = down.astype(BF16)

    @pl.when(step == pl.num_programs(0) - 1)
    def _():
        g_last[...] = acc[...].astype(BF16)
        to_neighbour([row], True, "wait")


def mid_back_body(
    per, q, totals, hook, lg, wl, mid, coef, sg, even, up, coef5, grads, halo, g_side, *scr
):
    acc, acc_s, rim, send, recv, *ex = scr
    step = pl.program_id(0)
    hook(-1)

    @pl.when(step == 0)
    def _():
        acc[...] = jnp.zeros_like(acc)
        acc_s[...] = jnp.zeros_like(acc_s)

    hook(0)
    for c in range(0, mid.shape[1], CHUNK):
        cols = slice(c, c + CHUNK)
        part = dot_nt(lg[...], wl[cols, :])
        normed = mid[:, cols] * coef[0:1, cols] + coef[1:2, cols]
        half = normed * coef[2:3, cols] + coef[3:4, cols]
        part = part * slope_twice(half, jnp.tanh(half))
        up[:, cols] = part
        rim[pl.ds(step * per, per), :, cols] = part.reshape(per, q, CHUNK)[:, 0:16].astype(BF16)
        acc[0:8, cols] += fold(part)
        acc[8:16, cols] += fold(part * normed)
    flat = even[...].reshape(per * q, even.shape[3])
    for c in range(0, sg.shape[1], CHUNK):
        cols = slice(c, c + CHUNK)
        acc_s[:, cols] += dot_tn(flat, sg[:, cols])
    to_neighbour([rim_copy(rim, halo, per, step, send, recv)], True, "start")

    @pl.when(step == pl.num_programs(0) - 1)
    def _():
        sums_out(ex[0], acc[0:8, :], acc[8:16, :])
        one = Exchange(ex)
        one.start()
        g_side[...] = acc_s[...].astype(BF16)
        one.turn()
        one.finish(totals, [coef], [coef5, grads])
        rim_finish(rim, halo, per, send, recv)


def conv_back_body(
    per, px, q, totals, hook, mup, mid, rim_up, rim_normed, pre, coef2, back, coef, w, *refs
):
    up, g_mid, coef6, grads, mg, mgs, acc, acc_g, wbd, *ex = refs
    hook(-1)
    step = pl.program_id(0)
    width = mid.shape[1]
    rows = per * q

    @pl.when(step == 0)
    def _():
        acc[...] = jnp.zeros_like(acc)
        acc_g[...] = jnp.zeros_like(acc_g)
        spread_weights(w, wbd)

    ext = q + 16
    below = lax.axis_index("height") < lax.axis_size("height") - 1
    last_col = lax.broadcasted_iota(jnp.int32, (rows, CHUNK), 0) % 16 == 15
    last_rim = lax.broadcasted_iota(jnp.int32, (per * 16, CHUNK), 0) % 16 == 15
    for c in range(0, width, CHUNK):
        cols = slice(c, c + CHUNK)
        hook(c // CHUNK)
        normed = mid[:, cols] * coef2[0:1, cols] + coef2[1:2, cols]
        grad = (mup[:, cols] * back[0:1, cols] + back[1:2, cols] + normed * back[2:3, cols]).astype(BF16)
        mg[:, 0:q, cols] = grad.reshape(per, q, CHUNK)
        grad = pltpu.roll(grad.astype(F32), rows - 1, 0)
        mgs[:, 0:q, cols] = jnp.where(last_col, 0.0, grad).astype(BF16).reshape(per, q, CHUNK)
        rim = rim_up[:, :, cols].astype(F32).reshape(per * 16, CHUNK) * back[0:1, cols] + back[1:2, cols]
        rim = rim + rim_normed[:, :, cols].astype(F32).reshape(per * 16, CHUNK) * back[2:3, cols]
        rim = jnp.where(below, rim, 0.0).astype(BF16)
        mg[:, q:ext, cols] = rim.reshape(per, 16, CHUNK)
        rim = pltpu.roll(rim.astype(F32), per * 16 - 1, 0)
        mgs[:, q:ext, cols] = jnp.where(last_rim, 0.0, rim).astype(BF16).reshape(per, 16, CHUNK)
        views = [ref[:, top : top + q, cols].reshape(rows, CHUNK) for top in (0, 16) for ref in (mg, mgs)]
        plans = (
            (0, ((1, 1, 0),)),
            (1, ((1, 2, 0), (1, 0, 1))),
            (2, ((2, 1, 0), (0, 1, 2))),
            (3, ((2, 2, 0), (2, 0, 1), (0, 2, 2), (0, 0, 3))),
        )
        for plane, taps in plans:
            total = None
            for row, col, view in taps:
                part = dot_nt(views[view], wbd[row * 3 + col, :, cols])
                total = part if total is None else total + part
            normed = pre[:, plane, :, cols].reshape(rows, CHUNK) * coef[0:1, cols] + coef[1:2, cols]
            half = normed * coef[2:3, cols] + coef[3:4, cols]
            th = jnp.tanh(half)
            act = (half + half * th).astype(BF16)
            total = total * slope_twice(half, th)
            up[:, plane, :, cols] = total.reshape(per, q, CHUNK).astype(BF16)
            acc[0:8, cols] += fold(total)
            acc[8:16, cols] += fold(total * normed)
            for row, col, view in taps:
                acc_g[row * 3 + col, :, cols] += dot_tn(act, views[view])

    @pl.when(step == pl.num_programs(0) - 1)
    def _():
        sums_out(ex[0], acc[0:8, :], acc[8:16, :])
        one = Exchange(ex)
        one.start()
        group = (lax.broadcasted_iota(jnp.int32, (32, width), 1) % CHUNK) // 32
        for tap in range(9):
            total = jnp.zeros((32, width), F32)
            for g in range(CHUNK // 32):
                total = total + jnp.where(group == g, acc_g[tap, g * 32 : (g + 1) * 32, :], 0.0)
            g_mid[tap] = total.astype(BF16)
        one.turn()
        one.finish(totals, [coef], [coef6, grads])


def first_grad(up, pre, coef, back, cols):
    normed = pre[:, cols] * coef[0:1, cols] + coef[1:2, cols]
    down = up[:, cols].astype(F32) * back[0:1, cols] + back[1:2, cols]
    return (down + normed * back[2:3, cols]).astype(BF16)


def first_back_body(hook, up, pre, coef, back, xp, g_first, acc):
    hook(-1)
    step = pl.program_id(0)

    @pl.when(step == 0)
    def _():
        acc[...] = jnp.zeros_like(acc)

    hook(0)
    for c in range(0, up.shape[1], CHUNK):
        cols = slice(c, c + CHUNK)
        acc[:, cols] += dot_tn(xp[...], first_grad(up, pre, coef, back, cols))

    @pl.when(step == pl.num_programs(0) - 1)
    def _():
        g_first[...] = acc[...].astype(BF16)


def image_back_body(per, px, q, hook, up, pre, coef, back, w1, sg, ws, out, fg, w1t, wst):
    hook(-1)
    step = pl.program_id(0)

    @pl.when(step == 0)
    def _():
        for c in range(0, w1.shape[0], CHUNK):
            cols = slice(c, c + CHUNK)
            w1t[:, cols] = w1[cols, :].T
            wst[:, cols] = ws[cols, :].T

    hook(0)
    for c in range(0, up.shape[1], CHUNK):
        cols = slice(c, c + CHUNK)
        fg[:, cols] = first_grad(up, pre, coef, back, cols)
    for c in range(0, w1.shape[0], CHUNK):
        cols = slice(c, c + CHUNK)
        side_back = dot(sg[...], wst[:, cols])
        part = dot(fg[...], w1t[:, cols])
        for k in range(per):
            even = part[k * px : k * px + q] + side_back[k * q : (k + 1) * q]
            out[k * px : k * px + q, cols] = even.astype(BF16)
            out[k * px + q : (k + 1) * px, cols] = part[k * px + q : (k + 1) * px].astype(BF16)


def place_body(px, planes, last, side, first, taps, wide_g, mid_g, first_g, *refs):
    out, last_out, side_out, first_out, taps_out = refs[:5]
    perm = refs[-1]

    @pl.when(pl.program_id(0) == 0)
    def _():
        perm[...] = planes_matrix(out.shape[1], out.shape[2], True)
        taps_out[...] = taps[...].astype(F32)
        rows = [first_g[1:2], first_g[0:1], mid_g[1:2], mid_g[0:1], wide_g[1:2], wide_g[0:1]]
        for ref, row in zip(refs[5:-1], rows + [wide_g[2:3], wide_g[0:1]]):
            ref[...] = row.reshape(ref.shape)

    for k in range(out.shape[0]):
        part = dot(perm[...], planes[k * px : (k + 1) * px, :]).astype(BF16)
        out[k] = part.reshape(out.shape[1:])
    last_out[...] = last[...].astype(F32)
    side_out[...] = side[...].astype(F32)
    first_out[...] = first[...].astype(F32)


def digit(axis, bit):
    return lax.rem(lax.div(lax.axis_index(axis), 1 << bit), 2)


def peer(axis, bit):
    batch, height = lax.axis_index("batch"), lax.axis_index("height")
    move = (1 - 2 * digit(axis, bit)) * (1 << bit)
    return (batch + move, height) if axis == "batch" else (batch, height + move)


def orders():
    bits_b = lax.axis_size("batch").bit_length() - 1
    bits_h = lax.axis_size("height").bit_length() - 1
    across = [("batch", k) for k in range(1, bits_b)]
    half = len(across) // 2
    x_bits, y_bits = across[:half], across[half:]
    z_bits = [("height", k) for k in range(bits_h)]
    return [x_bits + y_bits + z_bits, y_bits + x_bits + z_bits]


def stage_count():
    return len(orders()[0])


def lengths(rows):
    kept = [rows]
    for _ in range(stage_count()):
        kept.append(kept[-1] // 2 if kept[-1] % 32 == 0 else kept[-1])
    return kept


def landing(rows):
    return sum(lengths(rows)[1:])


def upper_lower():
    batch, height = lax.axis_index("batch"), lax.axis_index("height")
    size = lax.axis_size("height")
    return [(batch, lax.rem(height + 1, size)), (batch, lax.rem(height + size - 1, size))]


def partners():
    return [peer("batch", 0)] + [peer(axis, bit) for axis, bit in orders()[0]]


def remote(src, dst, send, recv, target):
    return pltpu.make_async_remote_copy(
        src_ref=src,
        dst_ref=dst,
        send_sem=send,
        recv_sem=recv,
        device_id=target,
        device_id_type=pl.DeviceIdType.MESH,
    )


class Flow:
    def __init__(self, rows, width, own, got, send, recv):
        self.own, self.got, self.send, self.recv = own, got, send, recv
        self.kept = lengths(rows)
        self.orders = orders()
        self.cols = [slice(0, width // 2), slice(width // 2, width)]
        self.low = []
        for order in self.orders:
            low = [0]
            for s, (axis, bit) in enumerate(order):
                move = digit(axis, bit) * self.kept[s + 1] if self.halved(s) else 0
                low.append(low[-1] + move)
            self.low.append(low)

    def halved(self, s):
        return self.kept[s + 1] < self.kept[s]

    def rows(self, first, count):
        return pl.ds(pl.multiple_of(first, 16), count)

    def keep(self, k, s):
        return self.rows(self.low[k][s], self.kept[s])

    def away(self, k, s):
        if not self.halved(s):
            return self.keep(k, s)
        axis, bit = self.orders[k][s]
        return self.rows(self.low[k][s] + (1 - digit(axis, bit)) * self.kept[s + 1], self.kept[s + 1])

    def place(self, s):
        return pl.ds(sum(self.kept[1 : s + 1]), self.kept[s + 1])

    def scatter(self, k, s):
        return remote(
            self.own.at[self.away(k, s), self.cols[k]],
            self.got.at[self.place(s), self.cols[k]],
            self.send.at[0, k, s],
            self.recv.at[0, k, s],
            peer(*self.orders[k][s]),
        )

    def scatter_start(self, s):
        for k in range(2):
            self.scatter(k, s).start()

    def scatter_finish(self, s):
        for k in range(2):
            self.scatter(k, s).wait()
            rows, cols = self.keep(k, s + 1), self.cols[k]
            total = self.own[rows, cols].astype(F32) + self.got[self.place(s), cols].astype(F32)
            self.own[rows, cols] = total.astype(BF16)

    def gather(self, k, s, rows):
        return remote(
            self.own.at[rows, self.cols[k]],
            self.own.at[rows, self.cols[k]],
            self.send.at[1, k, s],
            self.recv.at[1, k, s],
            peer(*self.orders[k][s]),
        )

    def gather_start(self, s):
        for k in range(2):
            if self.halved(s):
                self.gather(k, s, self.keep(k, s + 1)).start()

    def gather_finish(self, s):
        for k in range(2):
            if self.halved(s):
                self.gather(k, s, self.keep(k, s + 1)).wait_send()
                self.gather(k, s, self.away(k, s)).wait_recv()

    def moves(self, s, hbm, sems, out):
        copies = []
        for k in range(2):
            here = self.own.at[self.keep(k, s), self.cols[k]]
            there = hbm.at[self.keep(k, s), self.cols[k]]
            copies.append(pltpu.make_async_copy(*((here, there) if out else (there, here)), sems.at[k]))
        return copies


def run(copies, what):
    for copy in copies:
        getattr(copy, what)()


def own_half(ref):
    half = ref.shape[0] // 2
    return ref.at[pl.ds(pl.multiple_of(lax.axis_index("batch") % 2 * half, 16), half)]


def other_half(ref):
    half = ref.shape[0] // 2
    return ref.at[pl.ds(pl.multiple_of((1 - lax.axis_index("batch") % 2) * half, 16), half)]


def add_into(ref, other, step=64):
    for first in range(0, ref.shape[0], step):
        rows = slice(first, min(first + step, ref.shape[0]))
        ref[rows, :] = (ref[rows, :].astype(F32) + other[rows, :].astype(F32)).astype(BF16)


def carrying(body, counts, carry):
    def kernel(*refs):
        groups, first = [], 0
        for count in counts:
            groups.append(refs[first : first + count])
            first += count
        ins, c_ins, outs, c_outs, scr = groups
        c_scr = refs[first:]
        step = pl.program_id(0)
        points, last = carry(c_ins, c_outs, c_scr)

        def hook(point):
            for (when, where), action in points:
                if where == point:
                    pl.when(step == when)(action)

        body(hook, *ins, *outs, *scr)
        for action in last:
            pl.when(step == pl.num_programs(0) - 1)(action)

    return kernel


def carry_mid(c_ins, c_outs, c_scr):
    (g_last,) = c_ins
    (state_last,) = c_outs
    own, got, tmp, local, core, send, recv = c_scr
    flow = Flow(own.shape[0], own.shape[1], own, got, send, recv)
    load = pltpu.make_async_copy(own_half(g_last), own, local.at[0])
    copy = remote(other_half(g_last), tmp, core.at[0], core.at[1], peer("batch", 0))

    def start():
        load.start()
        signal_all()

    def enter():
        wait_all()
        copy.start()

    def first():
        load.wait()
        copy.wait()
        add_into(own, tmp)
        flow.scatter_start(0)

    def finish():
        flow.scatter_finish(0)
        dumps = flow.moves(1, state_last, local, True)
        run(dumps, "start")
        run(dumps, "wait")

    return [((0, -1), start), ((0, 0), enter), ((2, 0), first)], [finish]


def inner_stages(flow, done, first, until):
    stages = stage_count()

    def down(s):
        def action():
            flow.scatter_finish(s)
            if s + 1 < stages:
                flow.scatter_start(s + 1)
                return
            for k in range(2):
                rows = flow.keep(k, stages)
                done.own[rows, flow.cols[k]] = flow.own[rows, flow.cols[k]]
            done.gather_start(s)

        return action

    def back(s):
        def action():
            done.gather_finish(s)
            if s > until:
                done.gather_start(s - 1)

        return action

    return [down(s) for s in range(first, stages)] + [back(s) for s in range(stages - 1, until - 1, -1)]


def carry_conv(c_ins, c_outs, c_scr):
    state_last, g_side = c_ins
    part_last, state_side = c_outs
    own_l, got_l, full_l, own_s, got_s, tmp, local, core, send_l, recv_l, send_s, recv_s = c_scr
    rows, width = own_l.shape
    last = Flow(rows, width, own_l, got_l, send_l, recv_l)
    done = Flow(rows, width, full_l, None, send_l, recv_l)
    side = Flow(rows, width, own_s, got_s, send_s, recv_s)
    loads = last.moves(1, state_last, local, False)
    load = pltpu.make_async_copy(own_half(g_side), own_s, local.at[2])
    copy = remote(other_half(g_side), tmp, core.at[0], core.at[1], peer("batch", 0))
    inner = inner_stages(last, done, 1, 2)

    def start():
        run(loads, "start")
        load.start()
        signal_all()

    def enter():
        wait_all()
        run(loads, "wait")
        last.scatter_start(1)
        copy.start()

    def first_side():
        load.wait()
        copy.wait()
        add_into(own_s, tmp)
        side.scatter_start(0)

    def next_side(s):
        def action():
            side.scatter_finish(s)
            side.scatter_start(s + 1)

        return action

    def finish():
        side.scatter_finish(1)
        dumps = done.moves(2, part_last, local, True)
        dumps += side.moves(2, state_side, local.at[pl.ds(2, 2)], True)
        run(dumps, "start")
        run(dumps, "wait")

    points = [((0, -1), start), ((0, 0), enter), ((1, 0), first_side)]
    places = [(1, 2), (3, 0), (4, 1), (5, 2)]
    points += [(places[min(k, 3)], act) for k, act in enumerate(inner[:-1])]
    points += [((4, 0), next_side(0))]
    return points, [inner[-1], finish]


class Halves:
    def __init__(self, array, own, tmp, sems, core):
        mine, wide = lax.axis_index("batch") % 2, own.shape[1]
        self.own, self.tmp, self.rows = own, tmp, array.shape[0]
        self.cols = pl.ds(pl.multiple_of(mine * wide, LANES), wide)
        away = pl.ds(pl.multiple_of((1 - mine) * wide, LANES), wide)
        rows = slice(0, self.rows)
        self.load = pltpu.make_async_copy(array.at[:, self.cols], own.at[rows], sems.at[0])
        self.mate = remote(
            array.at[:, away], tmp.at[rows], core.at[0], core.at[1], peer("batch", 0)
        )

    def clear(self):
        left = (self.own.shape[0] - self.rows, self.own.shape[1])
        if left[0]:
            self.own[self.rows :, :] = jnp.zeros(left, BF16)
            self.tmp[self.rows :, :] = jnp.zeros(left, BF16)

    def add(self):
        self.load.wait()
        self.mate.wait()
        add_into(self.own, self.tmp)


def ends(src, dst, sem, core):
    return [
        pltpu.make_async_copy(src, dst, sem),
        remote(src, dst, core.at[0], core.at[1], peer("batch", 0)),
    ]


def carry_first(c_ins, c_outs, c_scr):
    part_last, state_side = c_ins
    half_last, part_side = c_outs
    own_l, own_s, got_s, full_s, local, send_l, recv_l, send_s, recv_s = c_scr
    rows, width = own_l.shape
    last = Flow(rows, width, own_l, None, send_l, recv_l)
    side = Flow(rows, width, own_s, got_s, send_s, recv_s)
    done_s = Flow(rows, width, full_s, None, send_s, recv_s)
    inner = inner_stages(side, done_s, 2, 3)
    loads = last.moves(2, part_last, local, False)
    loads += side.moves(2, state_side, local.at[pl.ds(2, 2)], False)

    def start():
        run(loads, "start")
        signal(partners())

    def enter():
        wait_partners()
        run(loads, "wait")
        last.gather_start(1)
        side.scatter_start(2)

    def next_last():
        last.gather_finish(1)
        last.gather_start(0)

    def finish():
        last.gather_finish(0)
        dumps = last.moves(0, half_last, local, True)
        dumps += done_s.moves(3, part_side, local.at[pl.ds(2, 2)], True)
        run(dumps, "start")
        run(dumps, "wait")

    points = [((0, -1), start), ((0, 0), enter), ((3, 0), next_last)]
    points += [((min(4 + 4 * k, 8), 0), act) for k, act in enumerate(inner[:-1])]
    return points, [inner[-1], finish]


def carry_image(c_ins, c_outs, c_scr):
    half_last, part_side, g_mid, g_first = c_ins
    all_last, all_side, all_first, all_mid = c_outs
    own_l, own_s, own_m, got_m, tmp_m, full_m, tmp_h, local, core = c_scr[:9]
    send_s, recv_s, send_m, recv_m = c_scr[9:13]
    side = Flow(own_s.shape[0], own_s.shape[1], own_s, None, send_s, recv_s)
    heads, dones = [], []
    for k in (13, 18):
        own_h, got_h, full_h, send_h, recv_h = c_scr[k : k + 5]
        heads.append(Flow(own_h.shape[0], own_h.shape[1], own_h, got_h, send_h, recv_h))
        dones.append(Flow(own_h.shape[0], own_h.shape[1], full_h, None, send_h, recv_h))
    heads.append(Flow(own_m.shape[0], own_m.shape[1], own_m, got_m, send_m, recv_m))
    dones.append(Flow(own_m.shape[0], own_m.shape[1], full_m, None, send_m, recv_m))
    halves = Halves(g_mid, own_m, tmp_m, local.at[pl.ds(5, 1)], core.at[pl.ds(6, 2)])
    few_h = c_scr[13].shape[0]
    parts_h = [slice(0, few_h), slice(few_h, 2 * few_h)]
    stages = stage_count()
    loads_h = [
        pltpu.make_async_copy(own_half(g_first).at[part], flow.own, local.at[7 + k])
        for k, (part, flow) in enumerate(zip(parts_h, heads))
    ]
    copy = remote(other_half(g_first), tmp_h, core.at[0], core.at[1], peer("batch", 0))
    loads = side.moves(3, part_side, local.at[pl.ds(3, 2)], False)
    few = slice(0, all_mid.shape[0])
    load_l = pltpu.make_async_copy(half_last, own_l, local.at[0])
    ends_last = ends(own_l, own_half(all_last), local.at[1], core.at[pl.ds(2, 2)])
    ends_side = ends(own_s, own_half(all_side), local.at[3], core.at[pl.ds(4, 2)])
    ends_head = []
    for k, (part, flow) in enumerate(zip(parts_h, dones)):
        pair = core.at[pl.ds(8 + 2 * k, 2)]
        ends_head.append(ends(flow.own, own_half(all_first).at[part], local.at[7 + k], pair))
    pair = core.at[pl.ds(12, 2)]
    ends_head.append(ends(full_m.at[few], all_mid.at[:, halves.cols], local.at[5], pair))

    def start():
        run(loads_h + loads + [load_l, halves.load], "start")
        halves.clear()
        signal(partners())

    def enter():
        wait_partners()
        copy.start()
        halves.mate.start()
        run(loads, "wait")
        side.gather_start(2)

    def first():
        run(loads_h, "wait")
        copy.wait()
        for part, flow in zip(parts_h, heads):
            add_into(flow.own, tmp_h.at[part])
            flow.scatter_start(0)
        halves.add()
        heads[2].scatter_start(0)
        load_l.wait()
        run(ends_last, "start")

    def back(flow, s, then):
        def action():
            flow.gather_finish(s)
            if s:
                flow.gather_start(s - 1)
            else:
                run(then, "start")

        return action

    def head_next(s):
        def action():
            for flow, done in zip(heads, dones):
                flow.scatter_finish(s)
                if s + 1 < stages:
                    flow.scatter_start(s + 1)
                    continue
                for k in range(2):
                    rows_k = flow.keep(k, stages)
                    done.own[rows_k, flow.cols[k]] = flow.own[rows_k, flow.cols[k]]
                done.gather_start(s)

        return action

    def head_back(s):
        def action():
            for done, end in zip(dones, ends_head):
                back(done, s, end)()

        return action

    def finish():
        for end in [ends_last, ends_side] + ends_head:
            run(end, "wait")

    points = [((0, -1), start), ((0, 0), enter), ((2, 0), first), ((4, 0), back(side, 2, None))]
    points += [((4, 0), head_next(0)), ((6, 0), head_next(1))]
    points += [((7, 0), back(side, 1, None))]
    places = [8, 10]
    points += [((places[min(s - 2, 1)], 0), head_next(s)) for s in range(2, stages)]
    tail = [head_back(s) for s in range(stages - 1, 1, -1)]
    tail += [back(side, 0, ends_side), head_back(1), head_back(0), finish]
    return points, tail


def per_device(
    images,
    w_first,
    gain_first,
    shift_first,
    w_mid,
    gain_mid,
    shift_mid,
    w_last,
    gain_last,
    shift_last,
    w_side,
    gain_side,
    shift_side,
    cotangent,
):
    n, rows_in, cols_in, cin = images.shape
    mid = w_first.shape[1]
    wide = w_last.shape[1]
    gw = w_mid.shape[2]
    rows_out, cols_out = rows_in // 2, cols_in // 2
    px, q = rows_in * cols_in, rows_out * cols_out
    devices = lax.axis_size("batch") * lax.axis_size("height")
    cells_in = float(n * px * devices)
    cells_out = float(n * q * devices)
    size_h = lax.axis_size("height")
    per = 4
    steps = n // per
    rows = per * q

    anywhere = pl.BlockSpec(memory_space=pl.ANY)
    dma = pltpu.SemaphoreType.DMA
    halo_x = lax.ppermute(images[:, rows_in - 1], "height", [(i, i + 1) for i in range(size_h - 1)])
    taps = w_mid.reshape(9, gw, mid)
    size_p = per * cols_in

    eights, wide_eights = whole((8, mid)), whole((8, wide))
    xp, pre, side_pre, coef1, side_coef = call(
        functools.partial(
            first_body, per, px, q, functools.partial(first_totals, cells_in, cells_out, mid, wide)
        ),
        "first_product",
        (steps,),
        [
            pl.BlockSpec((per, rows_in, cols_in, cin), lambda s: (s, 0, 0, 0)),
            whole((cin, mid)),
            whole((cin, wide)),
            whole((mid,)),
            whole((mid,)),
        ],
        [
            rows_spec(per * px, cin),
            rows_spec(per * px, mid),
            rows_spec(rows, wide),
            eights,
            wide_eights,
        ],
        [
            shape((n * px, cin), BF16),
            shape((n * px, mid)),
            shape((n * q, wide)),
            shape((8, mid)),
            shape((8, wide)),
        ],
        [pltpu.VMEM((16, mid), F32), pltpu.VMEM((16, wide), F32), pltpu.VMEM((px, px), BF16)]
        + exchange_scratch(2 * (mid + wide) // LANES),
        flops=2 * n * (px * cin * (mid + px) + q * cin * wide),
        moved=n * px * cin * 8 + n * q * wide * 4 + cin * (mid + wide) * 2,
        ident=6,
    )(images, w_first, w_side, gain_first, shift_first)

    pre_planes = pre.reshape(n, 4, q, mid)
    planes_spec = pl.BlockSpec((per, 4, q, mid), lambda s: (s, 0, 0, 0))
    mid_pre, coef2 = call(
        functools.partial(conv_body, per, px, q, functools.partial(mid_totals, cells_out, mid)),
        "grouped_conv",
        (steps,),
        [
            planes_spec,
            pl.BlockSpec((per, cols_in, cin), lambda s: (s, 0, 0)),
            whole((cin, mid)),
            eights,
            whole((9, gw, mid)),
            whole((mid,)),
            whole((mid,)),
        ],
        [rows_spec(rows, mid), eights],
        [shape((n * q, mid)), shape((8, mid))],
        [
            pltpu.VMEM((per, q, mid), BF16),
            pltpu.VMEM((per, q, mid), BF16),
            pltpu.VMEM((per, q + 16, mid), BF16),
            pltpu.VMEM((per, q + 16, mid), BF16),
            pltpu.VMEM((9, CHUNK, mid), BF16),
            pltpu.VMEM((size_p, size_p), BF16),
            pltpu.VMEM((16, mid), F32),
        ]
        + exchange_scratch(2 * mid // LANES),
        flops=2 * n * q * mid * CHUNK * 9 + 2 * n * cols_in * cin * mid,
        moved=n * px * mid * 4 + n * q * mid * 4,
        ident=0,
    )(pre_planes, halo_x, w_first, coef1, taps, gain_mid, shift_mid)

    rim_spec = pl.BlockSpec((per, cols_out, mid), lambda s: (s, 0, 0))
    rim_shape = shape((n, cols_out, mid), BF16)
    mid_act, last_pre, coef3, rim_own = call(
        functools.partial(last_body, per, q, functools.partial(last_totals, cells_out, wide)),
        "last_product",
        (steps,),
        [rows_spec(rows, mid), eights, whole((mid, wide))] + [whole((wide,))] * 4 + [wide_eights],
        [rows_spec(rows, mid), rows_spec(rows, wide), wide_eights, rim_spec],
        [shape((n * q, mid), BF16), shape((n * q, wide)), shape((8, wide)), rim_shape],
        [pltpu.VMEM((16, wide), F32)] + exchange_scratch(2 * wide // LANES),
        flops=2 * n * q * mid * wide,
        moved=n * q * (mid * 6 + wide * 4),
        ident=7,
    )(mid_pre, coef2, w_last, gain_last, shift_last, gain_side, shift_side, side_coef)

    cot = cotangent.reshape(n * q, wide)
    stat_rows = 3 * wide // LANES
    output, stat = call(
        out_body,
        "output",
        (steps,),
        [rows_spec(rows, wide), rows_spec(rows, wide), rows_spec(rows, wide), wide_eights],
        [rows_spec(rows, wide), whole((stat_rows, LANES))],
        [shape((n * q, wide), BF16), shape((stat_rows, LANES))],
        [pltpu.VMEM((24, wide), F32)],
        flops=30 * n * q * wide,
        moved=n * q * wide * 12,
    )(last_pre, side_pre, cot, coef3)

    xp_planes = xp.reshape(n, 4, q, cin)
    half_l = mid // 2
    stages = stage_count()
    sems = dma((2, 2, stages))
    state = shape((half_l, wide), BF16)
    buf = pltpu.VMEM((half_l, wide), BF16)
    got = pltpu.VMEM((landing(half_l), wide), BF16)
    last_grad, side_grad, g_last, wide_grads, rim_normed = call(
        functools.partial(last_grad_body, functools.partial(out_totals, cells_out, wide)),
        "last_gradients",
        (steps,),
        [
            rows_spec(rows, wide),
            rows_spec(rows, wide),
            rows_spec(rows, wide),
            wide_eights,
            rows_spec(rows, mid),
            whole((stat_rows, LANES)),
            anywhere,
        ],
        [rows_spec(rows, wide), rows_spec(rows, wide), whole((mid, wide)), wide_eights, anywhere],
        [
            shape((n * q, wide), BF16),
            shape((n * q, wide), BF16),
            shape((mid, wide), BF16),
            shape((8, wide)),
            rim_shape,
        ],
        [pltpu.VMEM((mid, wide), F32), pltpu.VMEM((8, wide), F32), dma, dma]
        + exchange_scratch(stat_rows),
        flops=2 * n * q * mid * wide,
        moved=n * q * (wide * 14 + mid * 2) + mid * wide * 2,
        ident=3,
    )(last_pre, side_pre, cot, coef3, mid_act, stat, rim_own)
    rims = [pltpu.VMEM((n, cols_out, mid), BF16), dma((steps,)), dma((steps,))]
    inner_scratch = exchange_scratch(2 * mid // LANES)
    mid_up, coef5, mid_grads, rim_up, g_side, state_last = call(
        carrying(
            functools.partial(mid_back_body, per, q, functools.partial(inner_totals, cells_out, mid)),
            (6, 1, 5, 1, 5 + len(inner_scratch)),
            carry_mid,
        ),
        "mid_back",
        (steps,),
        [
            rows_spec(rows, wide),
            whole((mid, wide)),
            rows_spec(rows, mid),
            eights,
            rows_spec(rows, wide),
            pl.BlockSpec((per, 1, q, cin), lambda s: (s, 0, 0, 0)),
            anywhere,
        ],
        [rows_spec(rows, mid), eights, eights, anywhere, whole((cin, wide)), anywhere],
        [
            shape((n * q, mid)),
            shape((8, mid)),
            shape((8, mid)),
            rim_shape,
            shape((cin, wide), BF16),
            state,
        ],
        [pltpu.VMEM((16, mid), F32), pltpu.VMEM((cin, wide), F32)]
        + rims
        + inner_scratch
        + [buf, got, buf, dma((2,)), dma((2,)), sems, sems],
        flops=2 * n * q * (mid + cin) * wide,
        moved=n * q * (wide * 4 + mid * 10) + mid * wide * 4,
        ident=9,
    )(last_grad, w_last, mid_pre, coef2, side_grad, xp_planes, g_last)

    first_up, g_mid, coef6, first_grads, part_last, state_side = call(
        carrying(
            functools.partial(
                conv_back_body, per, px, q, functools.partial(inner_totals, cells_in, mid)
            ),
            (9, 2, 4, 2, 5 + len(inner_scratch)),
            carry_conv,
        ),
        "grouped_conv_back",
        (steps,),
        [
            rows_spec(rows, mid),
            rows_spec(rows, mid),
            rim_spec,
            rim_spec,
            planes_spec,
            eights,
            eights,
            eights,
            whole((9, gw, mid)),
            anywhere,
            anywhere,
        ],
        [planes_spec, whole((9, gw, mid)), eights, eights, anywhere, anywhere],
        [
            shape((n, 4, q, mid), BF16),
            shape((9, gw, mid), BF16),
            shape((8, mid)),
            shape((8, mid)),
            state,
            state,
        ],
        [
            pltpu.VMEM((per, q + 16, mid), BF16),
            pltpu.VMEM((per, q + 16, mid), BF16),
            pltpu.VMEM((16, mid), F32),
            pltpu.VMEM((9, CHUNK, mid), F32),
            pltpu.VMEM((9, CHUNK, mid), BF16),
        ]
        + inner_scratch
        + [buf, got, buf, buf, got, buf, dma((4,)), dma((2,))]
        + [sems] * 4,
        flops=4 * n * q * mid * CHUNK * 9,
        moved=n * q * mid * 8 + n * px * mid * 6,
        vmem=60,
        ident=10,
    )(
        mid_up,
        mid_pre,
        rim_up,
        rim_normed,
        pre_planes,
        coef2,
        coef5,
        coef1,
        taps,
        state_last,
        g_side,
    )

    flat_up = first_up.reshape(n * px, mid)
    few = per // 2
    g_first, half_last, part_side = call(
        carrying(first_back_body, (5, 2, 1, 2, 1), carry_first),
        "first_gradient",
        (n // few,),
        [
            rows_spec(few * px, mid),
            rows_spec(few * px, mid),
            eights,
            eights,
            rows_spec(few * px, cin),
            anywhere,
            anywhere,
        ],
        [whole((cin, mid)), anywhere, anywhere],
        [shape((cin, mid), BF16), state, state],
        [pltpu.VMEM((cin, mid), F32), buf, buf, got, buf, dma((4,))] + [sems] * 4,
        flops=2 * n * px * mid * cin,
        moved=n * px * (mid * 6 + cin * 2),
        ident=11,
    )(flat_up, pre, coef1, coef6, xp, part_last, state_side)

    half_m = mid // 2
    unit = 16 * (devices // 2)
    taps_rows = -(-9 * gw // unit) * unit
    buf_m = pltpu.VMEM((taps_rows, half_m), BF16)
    got_m = pltpu.VMEM((landing(taps_rows), half_m), BF16)
    quarter = cin // 4
    buf_h = pltpu.VMEM((quarter, mid), BF16)
    got_h = pltpu.VMEM((landing(quarter), mid), BF16)
    planes, all_last, all_side, all_first, all_mid = call(
        carrying(functools.partial(image_back_body, few, px, q), (7, 4, 1, 4, 3), carry_image),
        "image_gradient",
        (n // few,),
        [
            rows_spec(few * px, mid),
            rows_spec(few * px, mid),
            eights,
            eights,
            whole((cin, mid)),
            rows_spec(few * q, wide),
            whole((cin, wide)),
        ]
        + [anywhere] * 4,
        [rows_spec(few * px, cin)] + [anywhere] * 4,
        [
            shape((n * px, cin), BF16),
            shape((mid, wide), BF16),
            shape((cin, wide), BF16),
            shape((cin, mid), BF16),
            shape((9 * gw, mid), BF16),
        ],
        [
            pltpu.VMEM((few * px, mid), BF16),
            pltpu.VMEM((mid, cin), BF16),
            pltpu.VMEM((wide, cin), BF16),
        ]
        + [buf, buf, buf_m, got_m, buf_m, buf_m, pltpu.VMEM((2 * quarter, mid), BF16)]
        + [dma((9,)), dma((14,))]
        + [sems] * 4
        + [buf_h, got_h, buf_h, sems, sems] * 2,
        flops=2 * n * px * cin * mid + 2 * n * q * cin * wide,
        moved=n * px * (mid * 6 + cin * 2) + n * q * wide * 2,
        ident=12,
    )(
        flat_up,
        pre,
        coef1,
        coef6,
        w_first,
        side_grad,
        w_side,
        half_last,
        part_side,
        g_mid.reshape(9 * gw, mid),
        g_first,
    )
    three = 3
    cuts = n // three
    vectors = [mid] * 4 + [wide] * 4
    grad_images, grad_last, grad_side, grad_first, grad_mid, *grad_vectors = call(
        functools.partial(place_body, px),
        "image_places",
        (cuts,),
        [
            rows_spec(three * px, cin),
            rows_spec(mid // cuts, wide),
            rows_spec(cin // cuts, wide),
            rows_spec(cin // cuts, mid),
            whole((9 * gw, mid)),
            wide_eights,
            eights,
            eights,
        ],
        [
            pl.BlockSpec((three, rows_in, cols_in, cin), lambda s: (s, 0, 0, 0)),
            rows_spec(mid // cuts, wide),
            rows_spec(cin // cuts, wide),
            rows_spec(cin // cuts, mid),
            whole((9 * gw, mid)),
        ]
        + [whole((k,)) for k in vectors],
        [
            shape((n, rows_in, cols_in, cin), BF16),
            shape((mid, wide)),
            shape((cin, wide)),
            shape((cin, mid)),
            shape((9 * gw, mid)),
        ]
        + [shape((k,)) for k in vectors],
        [pltpu.VMEM((px, px), BF16)],
        flops=2 * n * px * cin * px,
        moved=n * px * cin * 4 + (mid + cin) * wide * 6 + cin * mid * 6,
    )(planes, all_last, all_side, all_first, all_mid, wide_grads, mid_grads, first_grads)

    return (
        output.reshape(n, rows_out, cols_out, wide),
        grad_images,
        grad_first,
        grad_vectors[0],
        grad_vectors[1],
        grad_mid.reshape(3, 3, gw, mid),
        grad_vectors[2],
        grad_vectors[3],
        grad_last,
        grad_vectors[4],
        grad_vectors[5],
        grad_side,
        grad_vectors[6],
        grad_vectors[7],
    )


def solution(mesh):
    split = P("batch", "height", None, None)
    in_specs = (split,) + (P(),) * 12 + (split,)
    out_specs = (split, split) + (P(),) * 12
    return jax.shard_map(
        per_device, mesh=mesh, in_specs=in_specs, out_specs=out_specs, check_vma=False
    )
```

profile of v0, /device:TPU:0, one launch (start us, length us, event | category | flops | bytes accessed | tf_op | source)
XLA Modules:
  0.0 343.8 jit_solution(976793453769491957)
XLA Ops:
  0.6 1.6 slice_bitcast_fusion
  2.3 5.0 %collective-permute-start = (bf16[24,32,1024]{2,1,0:T(8,128)(2,1)S(1)}, bf16[24,32,1024]{2,1,0:T(8,128)(2,1)S(1)}, u32[]{:S(2)}, u32[]{:S(2)}) collective-permute-start(bf16[24,32,1024]{2,1,0:T(8,128)(2,1)S(1)} %slice_bitcast_fusion), channel_id=1, source_target_pairs={{0,1},{1,2},{2,3},{4,5},{5,6},{6,7},{8,9},{9,10},{10,11},{12,13},{... | collective-permute-start | bytes 4718600 | tf_op jit(solution)/shard_map/ppermute | solution.py:1157
  7.3 40.7 %first_product.1 = (bf16[6144,1024]{1,0:T(8,128)(2,1)}, f32[6144,1024]{1,0:T(8,128)}, f32[1536,2048]{1,0:T(8,128)}, f32[8,1024]{1,0:T(8,128)}, f32[8,2048]{1,0:T(8,128)}) custom-call(bf16[24,8,32,1024]{3,2,1,0:T(8,128)(2,1)} %img.1, bf16[1024,1024]{1,0:T(8,128)(2,1)} %refs_4_.1, bf16[1024,2048]{1,0:T(8,128)(2,1)} %refs_6_.1, f32[1024]{0:T(1024)} %gain.2, ...), custom_call_target="tpu_custom_call" | custom-call | flops 22548578304 | bytes 69206016 | tf_op jit(solution)/shard_map/first_product/pallas_call | solution.py:1162
  48.0 0.0 collective-permute-done.halo
  48.0 0.0 copy-start
  48.0 1.1 copy-done
  49.2 27.0 %grouped_conv.1 = (f32[1536,1024]{1,0:T(8,128)}, f32[8,1024]{1,0:T(8,128)}) custom-call(f32[24,4,64,1024]{3,2,1,0:T(8,128)} %bitcast.12, bf16[24,32,1024]{2,1,0:T(8,128)(2,1)} %copy-done, bf16[1024,1024]{1,0:T(8,128)(2,1)} %refs_4_.1, f32[8,1024]{1,0:T(8,128)} %get-tuple-element.66.coef.refs_7_.refs_2_, bf16[9,32,1024]{2,1,0:T(8,128)(2,1)} %bitcast.21, ...), custom_call_target="tpu_custom_call" | custom-call | flops 8858370048 | bytes 31457280 | tf_op jit(solution)/shard_map/grouped_conv/pallas_call | solution.py:1198
  76.2 20.0 %last_product.1 = (bf16[1536,1024]{1,0:T(8,128)(2,1)}, f32[1536,2048]{1,0:T(8,128)}, f32[8,2048]{1,0:T(8,128)}, bf16[24,16,1024]{2,1,0:T(8,128)(2,1)}) custom-call(f32[1536,1024]{1,0:T(8,128)} %get-tuple-element.67.mid.refs_2_.refs_1_, f32[8,1024]{1,0:T(8,128)} %get-tuple-element.68.coef.refs_3_.refs_5_, bf16[1024,2048]{1,0:T(8,128)(2,1)} %refs_1_.1, ...), custom_call_target="tpu_custom_call" | custom-call | flops 6442450944 | bytes 22020096 | tf_op jit(solution)/shard_map/last_product/pallas_call | solution.py:1230
  96.2 16.1 %output.1 = (bf16[1536,2048]{1,0:T(8,128)(2,1)}, f32[48,128]{1,0:T(8,128)}) custom-call(f32[1536,2048]{1,0:T(8,128)} %get-tuple-element.70.last, f32[1536,2048]{1,0:T(8,128)} %get-tuple-element.71.side, bf16[1536,2048]{1,0:T(8,128)(2,1)} %bitcast.14, f32[8,2048]{1,0:T(8,128)} %get-tuple-element.72.coef), custom_call_target="tpu_custom_call" | custom-call | flops 94371840 | bytes 37748736 | tf_op jit(solution)/shard_map/output/pallas_call | solution.py:1245
  112.3 37.1 %last_gradients.1 = (bf16[1536,2048]{1,0:T(8,128)(2,1)}, bf16[1536,2048]{1,0:T(8,128)(2,1)}, bf16[1024,2048]{1,0:T(8,128)(2,1)}, f32[8,2048]{1,0:T(8,128)}, bf16[24,16,1024]{2,1,0:T(8,128)(2,1)}) custom-call(f32[1536,2048]{1,0:T(8,128)} %get-tuple-element.70.last, f32[1536,2048]{1,0:T(8,128)} %get-tuple-element.71.side, bf16[1536,2048]{1,0:T(8,128)(2,1)} %bitcast.15, ...), custom_call_target="tpu_custom_call" | custom-call | flops 6442450944 | bytes 51380224 | tf_op jit(solution)/shard_map/last_gradients/pallas_call | solution.py:1264
  149.4 34.9 %mid_back.1 = (f32[1536,1024]{1,0:T(8,128)}, f32[8,1024]{1,0:T(8,128)}, f32[8,1024]{1,0:T(8,128)}, bf16[24,16,1024]{2,1,0:T(8,128)(2,1)}, bf16[1024,2048]{1,0:T(8,128)(2,1)}, /*index=5*/bf16[512,2048]{1,0:T(8,128)(2,1)}) custom-call(bf16[1536,2048]{1,0:T(8,128)(2,1)} %get-tuple-element.77.refs_0_, bf16[1024,2048]{1,0:T(8,128)(2,1)} %refs_1_.1, ...), custom_call_target="tpu_custom_call" | custom-call | flops 12884901888 | bytes 36700160 | tf_op jit(solution)/shard_map/mid_back/pallas_call | solution.py:1293
  184.2 46.4 %grouped_conv_back.1 = (bf16[24,4,64,1024]{3,2,1,0:T(8,128)(2,1)}, bf16[9,32,1024]{2,1,0:T(8,128)(2,1)}, f32[8,1024]{1,0:T(8,128)}, f32[8,1024]{1,0:T(8,128)}, b...) custom-call(f32[1536,1024]{1,0:T(8,128)} %get-tuple-element.81.refs_0_, ...), custom_call_target="tpu_custom_call" | custom-call | flops 14495514624 | bytes 50331648 | tf_op jit(solution)/shard_map/grouped_conv_back/pallas_call | solution.py:1328
  230.6 30.6 %first_gradient.1 = (bf16[1024,1024]{1,0:T(8,128)(2,1)}, bf16[512,2048]{1,0:T(8,128)(2,1)}, bf16[512,2048]{1,0:T(8,128)(2,1)}) custom-call(bf16[6144,1024]{1,0:T(8,128)(2,1)} %bitcast.17, f32[6144,1024]{1,0:T(8,128)} %get-tuple-element.65.refs_1_, f32[8,1024]{1,0:T(8,128)} %get-tuple-element.66.coef.refs_7_.refs_2_, f32[8,1024]{1,0:T(8,128)} %get-tuple-element.88.refs_3_, ...), custom_call_target="tpu_custom_call" | custom-call | flops 12884901888 | bytes 50331648 | tf_op jit(solution)/shard_map/first_gradient/pallas_call | solution.py:1390
  261.2 61.8 %image_gradient.1 = (bf16[6144,1024]{1,0:T(8,128)(2,1)}, bf16[1024,2048]{1,0:T(8,128)(2,1)}, bf16[1024,2048]{1,0:T(8,128)(2,1)}, bf16[1024,1024]{1,0:T(8,128)(2,1)}, bf16[288,1024]{1,0:T(8,128)(2,1)}) custom-call(bf16[6144,1024]{1,0:T(8,128)(2,1)} %bitcast.18, f32[6144,1024]{1,0:T(8,128)} %get-tuple-element.65.refs_1_, ...), custom_call_target="tpu_custom_call" | custom-call | flops 19327352832 | bytes 56623104 | tf_op jit(solution)/shard_map/image_gradient/pallas_call | solution.py:1419
  323.0 20.6 %image_places.1 = (bf16[24,8,32,1024]{3,2,1,0:T(8,128)(2,1)}, f32[1024,2048]{1,0:T(8,128)}, f32[1024,2048]{1,0:T(8,128)}, f32[1024,1024]{1,0:T(8,128)}, f32[288,...) custom-call(bf16[6144,1024]{1,0:T(8,128)(2,1)} %get-tuple-element.95, ...), custom_call_target="tpu_custom_call" | custom-call | flops 3221225472 | bytes 56623104 | tf_op jit(solution)/shard_map/image_places/pallas_call | solution.py:1469
Async XLA Ops:
  2.3 45.8 %collective-permute-start = (bf16[24,32,1024]{2,1,0:T(8,128)(2,1)S(1)}, bf16[24,32,1024]{2,1,0:T(8,128)(2,1)S(1)}, u32[]{:S(2)}, u32[]{:S(2)}) collective-permute-start(bf16[24,32,1024]{2,1,0:T(8,128)(2,1)S(1)} %slice_bitcast_fusion), channel_id=1, source_target_pairs={{0,1},{1,2},{2,3},{4,5},{5,6},{6,7},{8,9},{9,10},{10,11},{12,13},{... | collective-permute-start | bytes 4718600 | tf_op jit(solution)/shard_map/ppermute | solution.py:1157
  48.0 1.1 copy-start
where the time goes:
time: 344 us
  Pallas kernels  335 us (97%)
  starting transfers between devices  5.03 us (1%)
    pallas_call x1, Pallas kernels, per_device(): call(carrying(functools.partial(image_back_body, few, px, q), (7, 4, 1, 4...  61.8 us
    pallas_call x1, Pallas kernels, per_device(): call(carrying(functools.partial(conv_back_body, per, px, q, functools.par...  46.4 us
    pallas_call x1, Pallas kernels, per_device(): call(functools.partial(first_body, per, px, q, functools.partial(first_to...  40.7 us
    pallas_call x1, Pallas kernels, per_device(): call(functools.partial(last_grad_body, functools.partial(out_totals, cell...  37.1 us
    pallas_call x1, Pallas kernels, per_device(): call(carrying(functools.partial(mid_back_body, per, q, functools.partial(...  34.9 us
    pallas_call x1, Pallas kernels, per_device(): call(carrying(first_back_body, (5, 2, 1, 2, 1), carry_first), 'first_grad...  30.6 us
    pallas_call x1, Pallas kernels, per_device(): call(functools.partial(conv_body, per, px, q, functools.partial(mid_total...  27 us
    pallas_call x1, Pallas kernels, per_device(): call(functools.partial(place_body, px), 'image_places', (cuts,), [rows_sp...  20.6 us
  transfers between devices with their start and end apart: 1, of which 0 were waited for; matrix products, arithmetic and copies ran while one was open for 0% of the time, Pallas kernels for 12%

commit v1 on v0

--- a/solution.py
+++ b/solution.py
@@ -197,15 +197,15 @@
     ]
 
 
-def first_totals(cells_in, cells_out, width, wide, total, params, outs):
+def first_totals(cells_in, width, total, params, outs):
     gain, shift = as_row(params[0]), as_row(params[1])
     fill(outs[0], act_rows(*norm_terms(total, 0, width, cells_in), gain, shift))
-    fill(outs[1], list(norm_terms(total, 2 * width // LANES, wide, cells_out)))
-
-
-def mid_totals(cells_out, width, total, params, outs):
+
+
+def mid_totals(cells_out, width, wide, total, params, outs):
     gain, shift = as_row(params[0]), as_row(params[1])
     fill(outs[0], act_rows(*norm_terms(total, 0, width, cells_out), gain, shift))
+    fill(outs[1], list(norm_terms(total, 2 * width // LANES, wide, cells_out)))
 
 
 def last_totals(cells_out, wide, total, params, outs):
@@ -298,10 +298,11 @@
 
 
 def first_body(
-    per, px, q, totals, img, w1, ws, gain, shift, xp, pre, side, coef, side_coef, acc, acc_s, perm, *ex
+    per, px, q, totals, img, w1, ws, gain, shift, xp, pre, side, coef, side_stat, acc, acc_s, perm, evens, *ex
 ):
-    step = pl.program_id(0)
+    step, steps = pl.program_id(0), pl.num_programs(0) // 2
     mid, wide = w1.shape[1], ws.shape[1]
+    rows = per * q
 
     @pl.when(step == 0)
     def _():
@@ -310,32 +311,49 @@
         perm[...] = planes_matrix(img.shape[1], img.shape[2], False)
         signal_all()
 
-    for k in range(per):
-        flat = img[k].reshape(px, img.shape[3])
-        moved = dot(perm[...], flat).astype(BF16)
-        xp[k * px : (k + 1) * px, :] = moved
+    @pl.when(step < steps)
+    def _():
+        for k in range(per):
+            flat = img[k].reshape(px, img.shape[3])
+            xp[k * px : (k + 1) * px, :] = dot(perm[...], flat).astype(BF16)
+        even = jnp.concatenate([xp[k * px : k * px + q, :] for k in range(per)], axis=0)
+        evens[pl.ds(pl.multiple_of(step * rows, 16), rows), :] = even
         for c in range(0, mid, CHUNK):
             cols = slice(c, c + CHUNK)
-            part = dot(moved, w1[:, cols])
-            pre[k * px : (k + 1) * px, cols] = part
+            part = dot(xp[...], w1[:, cols])
+            pre[:, cols] = part
             acc[0:8, cols] += fold(part)
             acc[8:16, cols] += fold(part * part)
-    even = jnp.concatenate([xp[k * px : k * px + q, :] for k in range(per)], axis=0)
-    for c in range(0, wide, CHUNK):
-        cols = slice(c, c + CHUNK)
-        part = dot(even, ws[:, cols])
-        side[:, cols] = part
-        acc_s[0:8, cols] += fold(part)
-        acc_s[8:16, cols] += fold(part * part)
+
+    @pl.when(step == steps)
+    def _():
+        sums_out(ex[0], acc[0:8, :], acc[8:16, :])
+        wait_all()
+        Exchange(ex).start()
+
+    @pl.when(step == steps + 2)
+    def _():
+        Exchange(ex).turn()
+
+    @pl.when(step >= steps)
+    def _():
+        even = evens[pl.ds(pl.multiple_of((step - steps) * rows, 16), rows), :]
+        for c in range(0, wide, CHUNK):
+            cols = slice(c, c + CHUNK)
+            part = dot(even, ws[:, cols])
+            side[:, cols] = part
+            acc_s[0:8, cols] += fold(part)
+            acc_s[8:16, cols] += fold(part * part)
 
     @pl.when(step == pl.num_programs(0) - 1)
     def _():
-        sums_out(ex[0], acc[0:8, :], acc[8:16, :], acc_s[0:8, :], acc_s[8:16, :])
-        wait_all()
-        exchange(ex, totals, [gain, shift], [coef, side_coef])
-
-
-def conv_body(per, px, q, totals, pre, halo, w1, coef, w, gain, shift, mid, coef2, *scr):
+        sums_out(side_stat, acc_s[0:8, :], acc_s[8:16, :])
+        Exchange(ex).finish(totals, [gain, shift], [coef])
+
+
+def conv_body(
+    per, px, q, totals, pre, halo, w1, coef, w, gain, shift, side_stat, mid, coef2, side_coef, *scr
+):
     a00, a01, a10, a11, wbd, perm, acc, *ex = scr
     step = pl.program_id(0)
     width = w1.shape[1]
@@ -382,8 +400,9 @@
     @pl.when(step == pl.num_programs(0) - 1)
     def _():
         sums_out(ex[0], acc[0:8, :], acc[8:16, :])
+        ex[0][2 * width // LANES :, :] = side_stat[...]
         wait_all()
-        exchange(ex, totals, [gain, shift], [coef2])
+        exchange(ex, totals, [gain, shift], [coef2, side_coef])
 
 
 def last_body(per, q, totals, mid, coef, w, gl, sl, gs, ss, side_coef, act, pre, coef3, rim, acc, *ex):
@@ -485,7 +504,7 @@
     per, q, totals, hook, lg, wl, mid, coef, sg, even, up, coef5, grads, halo, g_side, *scr
 ):
     acc, acc_s, rim, send, recv, *ex = scr
-    step = pl.program_id(0)
+    step, steps = pl.program_id(0), pl.num_programs(0) // 2
     hook(-1)
 
     @pl.when(step == 0)
@@ -494,29 +513,38 @@
         acc_s[...] = jnp.zeros_like(acc_s)
 
     hook(0)
-    for c in range(0, mid.shape[1], CHUNK):
-        cols = slice(c, c + CHUNK)
-        part = dot_nt(lg[...], wl[cols, :])
-        normed = mid[:, cols] * coef[0:1, cols] + coef[1:2, cols]
-        half = normed * coef[2:3, cols] + coef[3:4, cols]
-        part = part * slope_twice(half, jnp.tanh(half))
-        up[:, cols] = part
-        rim[pl.ds(step * per, per), :, cols] = part.reshape(per, q, CHUNK)[:, 0:16].astype(BF16)
-        acc[0:8, cols] += fold(part)
-        acc[8:16, cols] += fold(part * normed)
-    flat = even[...].reshape(per * q, even.shape[3])
-    for c in range(0, sg.shape[1], CHUNK):
-        cols = slice(c, c + CHUNK)
-        acc_s[:, cols] += dot_tn(flat, sg[:, cols])
-    to_neighbour([rim_copy(rim, halo, per, step, send, recv)], True, "start")
+
+    @pl.when(step < steps)
+    def _():
+        for c in range(0, mid.shape[1], CHUNK):
+            cols = slice(c, c + CHUNK)
+            part = dot_nt(lg[...], wl[cols, :])
+            normed = mid[:, cols] * coef[0:1, cols] + coef[1:2, cols]
+            half = normed * coef[2:3, cols] + coef[3:4, cols]
+            part = part * slope_twice(half, jnp.tanh(half))
+            up[:, cols] = part
+            rim[pl.ds(step * per, per), :, cols] = part.reshape(per, q, CHUNK)[:, 0:16].astype(BF16)
+            acc[0:8, cols] += fold(part)
+            acc[8:16, cols] += fold(part * normed)
+        to_neighbour([rim_copy(rim, halo, per, step, send, recv)], True, "start")
+
+    @pl.when(step == steps)
+    def _():
+        sums_out(ex[0], acc[0:8, :], acc[8:16, :])
+        Exchange(ex).start()
+
+    @pl.when(step >= steps)
+    def _():
+        flat = even[...].reshape(per * q, even.shape[3])
+        for c in range(0, sg.shape[1], CHUNK):
+            cols = slice(c, c + CHUNK)
+            acc_s[:, cols] += dot_tn(flat, sg[:, cols])
 
     @pl.when(step == pl.num_programs(0) - 1)
     def _():
-        sums_out(ex[0], acc[0:8, :], acc[8:16, :])
         one = Exchange(ex)
-        one.start()
+        one.turn()
         g_side[...] = acc_s[...].astype(BF16)
-        one.turn()
         one.finish(totals, [coef], [coef5, grads])
         rim_finish(rim, halo, per, send, recv)
 
@@ -598,11 +626,11 @@
     return (down + normed * back[2:3, cols]).astype(BF16)
 
 
-def first_back_body(hook, up, pre, coef, back, xp, g_first, acc):
+def first_back_body(hook, up, pre, coef, back, xp, g_near, g_far, acc):
     hook(-1)
-    step = pl.program_id(0)
-
-    @pl.when(step == 0)
+    step, steps = pl.program_id(0), pl.num_programs(0) // 2
+
+    @pl.when(lax.rem(step, steps) == 0)
     def _():
         acc[...] = jnp.zeros_like(acc)
 
@@ -611,9 +639,13 @@
         cols = slice(c, c + CHUNK)
         acc[:, cols] += dot_tn(xp[...], first_grad(up, pre, coef, back, cols))
 
-    @pl.when(step == pl.num_programs(0) - 1)
-    def _():
-        g_first[...] = acc[...].astype(BF16)
+    @pl.when(step == steps - 1)
+    def _():
+        g_near[...] = acc[...].astype(BF16)
+
+    @pl.when(step == 2 * steps - 1)
+    def _():
+        g_far[...] = acc[...].astype(BF16)
 
 
 def image_back_body(per, px, q, hook, up, pre, coef, back, w1, sg, ws, out, fg, w1t, wst):
@@ -641,7 +673,7 @@
             out[k * px + q : (k + 1) * px, cols] = part[k * px + q : (k + 1) * px].astype(BF16)
 
 
-def place_body(px, planes, last, side, first, taps, wide_g, mid_g, first_g, *refs):
+def place_body(px, planes, last, side, near, far, taps, wide_g, mid_g, first_g, *refs):
     out, last_out, side_out, first_out, taps_out = refs[:5]
     perm = refs[-1]
 
@@ -658,7 +690,9 @@
         out[k] = part.reshape(out.shape[1:])
     last_out[...] = last[...].astype(F32)
     side_out[...] = side[...].astype(F32)
-    first_out[...] = first[...].astype(F32)
+    half = near.shape[1]
+    first_out[:, :half] = near[...].astype(F32)
+    first_out[:, half:] = far[...].astype(F32)
 
 
 def digit(axis, bit):
@@ -828,7 +862,7 @@
         ins, c_ins, outs, c_outs, scr = groups
         c_scr = refs[first:]
         step = pl.program_id(0)
-        points, last = carry(c_ins, c_outs, c_scr)
+        points, last = carry(c_ins, c_outs, c_scr, outs)
 
         def hook(point):
             for (when, where), action in points:
@@ -842,7 +876,7 @@
     return kernel
 
 
-def carry_mid(c_ins, c_outs, c_scr):
+def carry_mid(c_ins, c_outs, c_scr, outs):
     (g_last,) = c_ins
     (state_last,) = c_outs
     own, got, tmp, local, core, send, recv = c_scr
@@ -870,7 +904,7 @@
         run(dumps, "start")
         run(dumps, "wait")
 
-    return [((0, -1), start), ((0, 0), enter), ((2, 0), first)], [finish]
+    return [((0, -1), start), ((0, 0), enter), ((3, 0), first)], [finish]
 
 
 def inner_stages(flow, done, first, until):
@@ -900,7 +934,7 @@
     return [down(s) for s in range(first, stages)] + [back(s) for s in range(stages - 1, until - 1, -1)]
 
 
-def carry_conv(c_ins, c_outs, c_scr):
+def carry_conv(c_ins, c_outs, c_scr, outs):
     state_last, g_side = c_ins
     part_last, state_side = c_outs
     own_l, got_l, full_l, own_s, got_s, tmp, local, core, send_l, recv_l, send_s, recv_s = c_scr
@@ -982,17 +1016,21 @@
     ]
 
 
-def carry_first(c_ins, c_outs, c_scr):
+def carry_first(c_ins, c_outs, c_scr, outs):
     part_last, state_side = c_ins
-    half_last, part_side = c_outs
-    own_l, own_s, got_s, full_s, local, send_l, recv_l, send_s, recv_s = c_scr
+    half_last, part_side, state_near = c_outs
+    own_l, own_s, got_s, full_s, local, send_l, recv_l, send_s, recv_s = c_scr[:9]
+    own_h, got_h, tmp_h, core, send_h, recv_h = c_scr[9:]
     rows, width = own_l.shape
     last = Flow(rows, width, own_l, None, send_l, recv_l)
     side = Flow(rows, width, own_s, got_s, send_s, recv_s)
     done_s = Flow(rows, width, full_s, None, send_s, recv_s)
+    head = Flow(own_h.shape[0], own_h.shape[1], own_h, got_h, send_h, recv_h)
     inner = inner_stages(side, done_s, 2, 3)
     loads = last.moves(2, part_last, local, False)
     loads += side.moves(2, state_side, local.at[pl.ds(2, 2)], False)
+    load = pltpu.make_async_copy(own_half(outs[0]), own_h, local.at[4])
+    copy = remote(other_half(outs[0]), tmp_h, core.at[0], core.at[1], peer("batch", 0))
 
     def start():
         run(loads, "start")
@@ -1008,54 +1046,62 @@
         last.gather_finish(1)
         last.gather_start(0)
 
+    def head_core():
+        load.start()
+        copy.start()
+
+    def head_first():
+        load.wait()
+        copy.wait()
+        add_into(own_h, tmp_h)
+        head.scatter_start(0)
+
     def finish():
         last.gather_finish(0)
+        head.scatter_finish(0)
         dumps = last.moves(0, half_last, local, True)
         dumps += done_s.moves(3, part_side, local.at[pl.ds(2, 2)], True)
+        dumps += head.moves(1, state_near, local.at[pl.ds(4, 2)], True)
         run(dumps, "start")
         run(dumps, "wait")
 
     points = [((0, -1), start), ((0, 0), enter), ((3, 0), next_last)]
     points += [((min(4 + 4 * k, 8), 0), act) for k, act in enumerate(inner[:-1])]
+    points += [((6, 0), head_core), ((8, 0), head_first)]
     return points, [inner[-1], finish]
 
 
-def carry_image(c_ins, c_outs, c_scr):
-    half_last, part_side, g_mid, g_first = c_ins
-    all_last, all_side, all_first, all_mid = c_outs
+def carry_image(c_ins, c_outs, c_scr, outs):
+    half_last, part_side, g_mid, state_near, g_far = c_ins
+    all_last, all_side, all_near, all_far, all_mid = c_outs
     own_l, own_s, own_m, got_m, tmp_m, full_m, tmp_h, local, core = c_scr[:9]
     send_s, recv_s, send_m, recv_m = c_scr[9:13]
+    near, got_n, full_n, send_n, recv_n = c_scr[13:18]
+    far, got_f, full_f, send_f, recv_f = c_scr[18:]
+
+    def pair(own, got, full, send, recv):
+        first = Flow(own.shape[0], own.shape[1], own, got, send, recv)
+        return first, Flow(own.shape[0], own.shape[1], full, None, send, recv)
+
     side = Flow(own_s.shape[0], own_s.shape[1], own_s, None, send_s, recv_s)
-    heads, dones = [], []
-    for k in (13, 18):
-        own_h, got_h, full_h, send_h, recv_h = c_scr[k : k + 5]
-        heads.append(Flow(own_h.shape[0], own_h.shape[1], own_h, got_h, send_h, recv_h))
-        dones.append(Flow(own_h.shape[0], own_h.shape[1], full_h, None, send_h, recv_h))
-    heads.append(Flow(own_m.shape[0], own_m.shape[1], own_m, got_m, send_m, recv_m))
-    dones.append(Flow(own_m.shape[0], own_m.shape[1], full_m, None, send_m, recv_m))
+    flow_n, done_n = pair(near, got_n, full_n, send_n, recv_n)
+    flow_f, done_f = pair(far, got_f, full_f, send_f, recv_f)
+    flow_m, done_m = pair(own_m, got_m, full_m, send_m, recv_m)
     halves = Halves(g_mid, own_m, tmp_m, local.at[pl.ds(5, 1)], core.at[pl.ds(6, 2)])
-    few_h = c_scr[13].shape[0]
-    parts_h = [slice(0, few_h), slice(few_h, 2 * few_h)]
-    stages = stage_count()
-    loads_h = [
-        pltpu.make_async_copy(own_half(g_first).at[part], flow.own, local.at[7 + k])
-        for k, (part, flow) in enumerate(zip(parts_h, heads))
-    ]
-    copy = remote(other_half(g_first), tmp_h, core.at[0], core.at[1], peer("batch", 0))
+    load_l = pltpu.make_async_copy(half_last, own_l, local.at[0])
+    load_f = pltpu.make_async_copy(own_half(g_far), far, local.at[9])
+    copy = remote(other_half(g_far), tmp_h, core.at[0], core.at[1], peer("batch", 0))
     loads = side.moves(3, part_side, local.at[pl.ds(3, 2)], False)
+    loads += flow_n.moves(1, state_near, local.at[pl.ds(7, 2)], False)
     few = slice(0, all_mid.shape[0])
-    load_l = pltpu.make_async_copy(half_last, own_l, local.at[0])
     ends_last = ends(own_l, own_half(all_last), local.at[1], core.at[pl.ds(2, 2)])
     ends_side = ends(own_s, own_half(all_side), local.at[3], core.at[pl.ds(4, 2)])
-    ends_head = []
-    for k, (part, flow) in enumerate(zip(parts_h, dones)):
-        pair = core.at[pl.ds(8 + 2 * k, 2)]
-        ends_head.append(ends(flow.own, own_half(all_first).at[part], local.at[7 + k], pair))
-    pair = core.at[pl.ds(12, 2)]
-    ends_head.append(ends(full_m.at[few], all_mid.at[:, halves.cols], local.at[5], pair))
+    ends_n = ends(full_n, own_half(all_near), local.at[7], core.at[pl.ds(8, 2)])
+    ends_f = ends(full_f, own_half(all_far), local.at[9], core.at[pl.ds(10, 2)])
+    ends_m = ends(full_m.at[few], all_mid.at[:, halves.cols], local.at[5], core.at[pl.ds(12, 2)])
 
     def start():
-        run(loads_h + loads + [load_l, halves.load], "start")
+        run(loads + [load_l, load_f, halves.load], "start")
         halves.clear()
         signal(partners())
 
@@ -1064,62 +1110,58 @@
         copy.start()
         halves.mate.start()
         run(loads, "wait")
+        flow_n.scatter_start(1)
         side.gather_start(2)
 
     def first():
-        run(loads_h, "wait")
+        load_f.wait()
         copy.wait()
-        for part, flow in zip(parts_h, heads):
-            add_into(flow.own, tmp_h.at[part])
-            flow.scatter_start(0)
+        add_into(far, tmp_h)
+        flow_f.scatter_start(0)
         halves.add()
-        heads[2].scatter_start(0)
+        flow_m.scatter_start(0)
         load_l.wait()
         run(ends_last, "start")
 
-    def back(flow, s, then):
+    def side_next(s):
         def action():
-            flow.gather_finish(s)
+            side.gather_finish(s)
             if s:
-                flow.gather_start(s - 1)
+                side.gather_start(s - 1)
             else:
-                run(then, "start")
+                run(ends_side, "start")
 
         return action
 
-    def head_next(s):
+    def chain(flow, done, stage, end):
+        actions = inner_stages(flow, done, stage, 0)
+        return actions + [lambda: run(end, "start")]
+
+    def both(one, two):
         def action():
-            for flow, done in zip(heads, dones):
-                flow.scatter_finish(s)
-                if s + 1 < stages:
-                    flow.scatter_start(s + 1)
-                    continue
-                for k in range(2):
-                    rows_k = flow.keep(k, stages)
-                    done.own[rows_k, flow.cols[k]] = flow.own[rows_k, flow.cols[k]]
-                done.gather_start(s)
+            one()
+            two()
 
         return action
 
-    def head_back(s):
-        def action():
-            for done, end in zip(dones, ends_head):
-                back(done, s, end)()
-
-        return action
-
     def finish():
-        for end in [ends_last, ends_side] + ends_head:
+        for end in (ends_last, ends_side, ends_n, ends_f, ends_m):
             run(end, "wait")
 
-    points = [((0, -1), start), ((0, 0), enter), ((2, 0), first), ((4, 0), back(side, 2, None))]
-    points += [((4, 0), head_next(0)), ((6, 0), head_next(1))]
-    points += [((7, 0), back(side, 1, None))]
-    places = [8, 10]
-    points += [((places[min(s - 2, 1)], 0), head_next(s)) for s in range(2, stages)]
-    tail = [head_back(s) for s in range(stages - 1, 1, -1)]
-    tail += [back(side, 0, ends_side), head_back(1), head_back(0), finish]
-    return points, tail
+    chain_n = chain(flow_n, done_n, 1, ends_n)
+    chain_f = chain(flow_f, done_f, 0, ends_f)
+    chain_m = chain(flow_m, done_m, 0, ends_m)
+    chain_f = [both(one, two) for one, two in zip(chain_f, chain_m)]
+    points = [((0, -1), start), ((0, 0), enter), ((1, 0), first)]
+    points += [((2 + 2 * k, 0), act) for k, act in enumerate(chain_n[:5])]
+    points += [((3 + 2 * k, 0), act) for k, act in enumerate(chain_f[:5])]
+    points += [((3, 0), side_next(2)), ((6, 0), side_next(1))]
+    tail, rest_n, rest_f = [], chain_n[5:], chain_f[5:]
+    for k in range(max(len(rest_n), len(rest_f))):
+        tail += rest_n[k : k + 1] + rest_f[k : k + 1]
+        if k == 1:
+            tail.append(side_next(0))
+    return points, tail + [finish]
 
 
 def per_device(
@@ -1159,35 +1201,48 @@
     size_p = per * cols_in
 
     eights, wide_eights = whole((8, mid)), whole((8, wide))
-    xp, pre, side_pre, coef1, side_coef = call(
+    def early(s):
+        return jnp.minimum(s, steps - 1)
+
+    def late(s):
+        return jnp.maximum(s - steps, 0)
+
+    def early_rows(count, cols):
+        return pl.BlockSpec((count, cols), lambda s: (early(s), 0))
+
+    def late_rows(count, cols):
+        return pl.BlockSpec((count, cols), lambda s: (late(s), 0))
+
+    xp, pre, side_pre, coef1, side_stat = call(
         functools.partial(
-            first_body, per, px, q, functools.partial(first_totals, cells_in, cells_out, mid, wide)
+            first_body, per, px, q, functools.partial(first_totals, cells_in, mid)
         ),
         "first_product",
-        (steps,),
-        [
-            pl.BlockSpec((per, rows_in, cols_in, cin), lambda s: (s, 0, 0, 0)),
+        (2 * steps,),
+        [
+            pl.BlockSpec((per, rows_in, cols_in, cin), lambda s: (early(s), 0, 0, 0)),
             whole((cin, mid)),
             whole((cin, wide)),
             whole((mid,)),
             whole((mid,)),
         ],
         [
-            rows_spec(per * px, cin),
-            rows_spec(per * px, mid),
-            rows_spec(rows, wide),
+            early_rows(per * px, cin),
+            early_rows(per * px, mid),
+            late_rows(rows, wide),
             eights,
-            wide_eights,
+            whole((2 * wide // LANES, LANES)),
         ],
         [
             shape((n * px, cin), BF16),
             shape((n * px, mid)),
             shape((n * q, wide)),
             shape((8, mid)),
-            shape((8, wide)),
+            shape((2 * wide // LANES, LANES)),
         ],
         [pltpu.VMEM((16, mid), F32), pltpu.VMEM((16, wide), F32), pltpu.VMEM((px, px), BF16)]
-        + exchange_scratch(2 * (mid + wide) // LANES),
+        + [pltpu.VMEM((n * q, cin), BF16)]
+        + exchange_scratch(2 * mid // LANES),
         flops=2 * n * (px * cin * (mid + px) + q * cin * wide),
         moved=n * px * cin * 8 + n * q * wide * 4 + cin * (mid + wide) * 2,
         ident=6,
@@ -1195,8 +1250,8 @@
 
     pre_planes = pre.reshape(n, 4, q, mid)
     planes_spec = pl.BlockSpec((per, 4, q, mid), lambda s: (s, 0, 0, 0))
-    mid_pre, coef2 = call(
-        functools.partial(conv_body, per, px, q, functools.partial(mid_totals, cells_out, mid)),
+    mid_pre, coef2, side_coef = call(
+        functools.partial(conv_body, per, px, q, functools.partial(mid_totals, cells_out, mid, wide)),
         "grouped_conv",
         (steps,),
         [
@@ -1207,9 +1262,10 @@
             whole((9, gw, mid)),
             whole((mid,)),
             whole((mid,)),
+            whole((2 * wide // LANES, LANES)),
         ],
-        [rows_spec(rows, mid), eights],
-        [shape((n * q, mid)), shape((8, mid))],
+        [rows_spec(rows, mid), eights, wide_eights],
+        [shape((n * q, mid)), shape((8, mid)), shape((8, wide))],
         [
             pltpu.VMEM((per, q, mid), BF16),
             pltpu.VMEM((per, q, mid), BF16),
@@ -1219,11 +1275,11 @@
             pltpu.VMEM((size_p, size_p), BF16),
             pltpu.VMEM((16, mid), F32),
         ]
-        + exchange_scratch(2 * mid // LANES),
+        + exchange_scratch(2 * (mid + wide) // LANES),
         flops=2 * n * q * mid * CHUNK * 9 + 2 * n * cols_in * cin * mid,
         moved=n * px * mid * 4 + n * q * mid * 4,
         ident=0,
-    )(pre_planes, halo_x, w_first, coef1, taps, gain_mid, shift_mid)
+    )(pre_planes, halo_x, w_first, coef1, taps, gain_mid, shift_mid, side_stat)
 
     rim_spec = pl.BlockSpec((per, cols_out, mid), lambda s: (s, 0, 0))
     rim_shape = shape((n, cols_out, mid), BF16)
@@ -1297,17 +1353,17 @@
             carry_mid,
         ),
         "mid_back",
-        (steps,),
-        [
-            rows_spec(rows, wide),
+        (2 * steps,),
+        [
+            early_rows(rows, wide),
             whole((mid, wide)),
-            rows_spec(rows, mid),
+            early_rows(rows, mid),
             eights,
-            rows_spec(rows, wide),
-            pl.BlockSpec((per, 1, q, cin), lambda s: (s, 0, 0, 0)),
+            late_rows(rows, wide),
+            pl.BlockSpec((per, 1, q, cin), lambda s: (late(s), 0, 0, 0)),
             anywhere,
         ],
-        [rows_spec(rows, mid), eights, eights, anywhere, whole((cin, wide)), anywhere],
+        [early_rows(rows, mid), eights, eights, anywhere, whole((cin, wide)), anywhere],
         [
             shape((n * q, mid)),
             shape((8, mid)),
@@ -1387,37 +1443,42 @@
 
     flat_up = first_up.reshape(n * px, mid)
     few = per // 2
-    g_first, half_last, part_side = call(
-        carrying(first_back_body, (5, 2, 1, 2, 1), carry_first),
+    half_m = mid // 2
+    half_h = cin // 2
+    kept_h = shape((half_h, half_m), BF16)
+    buf_h = pltpu.VMEM((half_h, half_m), BF16)
+    got_h = pltpu.VMEM((landing(half_h), half_m), BF16)
+    part_spec = pl.BlockSpec((per * px, half_m), lambda s: (lax.rem(s, steps), lax.div(s, steps)))
+    rows_part = pl.BlockSpec((8, half_m), lambda s: (0, lax.div(s, steps)))
+    g_near, g_far, half_last, part_side, state_near = call(
+        carrying(first_back_body, (5, 2, 2, 3, 1), carry_first),
         "first_gradient",
-        (n // few,),
-        [
-            rows_spec(few * px, mid),
-            rows_spec(few * px, mid),
-            eights,
-            eights,
-            rows_spec(few * px, cin),
+        (2 * steps,),
+        [
+            part_spec,
+            part_spec,
+            rows_part,
+            rows_part,
+            pl.BlockSpec((per * px, cin), lambda s: (lax.rem(s, steps), 0)),
             anywhere,
             anywhere,
         ],
-        [whole((cin, mid)), anywhere, anywhere],
-        [shape((cin, mid), BF16), state, state],
-        [pltpu.VMEM((cin, mid), F32), buf, buf, got, buf, dma((4,))] + [sems] * 4,
+        [whole((cin, half_m)), whole((cin, half_m))] + [anywhere] * 3,
+        [shape((cin, half_m), BF16), shape((cin, half_m), BF16), state, state, kept_h],
+        [pltpu.VMEM((cin, half_m), F32), buf, buf, got, buf, dma((6,))]
+        + [sems] * 4
+        + [buf_h, got_h, buf_h, dma((2,)), sems, sems],
         flops=2 * n * px * mid * cin,
-        moved=n * px * (mid * 6 + cin * 2),
+        moved=n * px * (mid * 6 + cin * 4),
         ident=11,
     )(flat_up, pre, coef1, coef6, xp, part_last, state_side)
 
-    half_m = mid // 2
     unit = 16 * (devices // 2)
     taps_rows = -(-9 * gw // unit) * unit
     buf_m = pltpu.VMEM((taps_rows, half_m), BF16)
     got_m = pltpu.VMEM((landing(taps_rows), half_m), BF16)
-    quarter = cin // 4
-    buf_h = pltpu.VMEM((quarter, mid), BF16)
-    got_h = pltpu.VMEM((landing(quarter), mid), BF16)
-    planes, all_last, all_side, all_first, all_mid = call(
-        carrying(functools.partial(image_back_body, few, px, q), (7, 4, 1, 4, 3), carry_image),
+    planes, all_last, all_side, all_near, all_far, all_mid = call(
+        carrying(functools.partial(image_back_body, few, px, q), (7, 5, 1, 5, 3), carry_image),
         "image_gradient",
         (n // few,),
         [
@@ -1429,13 +1490,14 @@
             rows_spec(few * q, wide),
             whole((cin, wide)),
         ]
-        + [anywhere] * 4,
-        [rows_spec(few * px, cin)] + [anywhere] * 4,
+        + [anywhere] * 5,
+        [rows_spec(few * px, cin)] + [anywhere] * 5,
         [
             shape((n * px, cin), BF16),
             shape((mid, wide), BF16),
             shape((cin, wide), BF16),
-            shape((cin, mid), BF16),
+            shape((cin, half_m), BF16),
+            shape((cin, half_m), BF16),
             shape((9 * gw, mid), BF16),
         ],
         [
@@ -1443,8 +1505,8 @@
             pltpu.VMEM((mid, cin), BF16),
             pltpu.VMEM((wide, cin), BF16),
         ]
-        + [buf, buf, buf_m, got_m, buf_m, buf_m, pltpu.VMEM((2 * quarter, mid), BF16)]
-        + [dma((9,)), dma((14,))]
+        + [buf, buf, buf_m, got_m, buf_m, buf_m, buf_h]
+        + [dma((10,)), dma((14,))]
         + [sems] * 4
         + [buf_h, got_h, buf_h, sems, sems] * 2,
         flops=2 * n * px * cin * mid + 2 * n * q * cin * wide,
@@ -1461,7 +1523,8 @@
         half_last,
         part_side,
         g_mid.reshape(9 * gw, mid),
-        g_first,
+        state_near,
+        g_far,
     )
     three = 3
     cuts = n // three
@@ -1474,7 +1537,8 @@
             rows_spec(three * px, cin),
             rows_spec(mid // cuts, wide),
             rows_spec(cin // cuts, wide),
-            rows_spec(cin // cuts, mid),
+            rows_spec(cin // cuts, half_m),
+            rows_spec(cin // cuts, half_m),
             whole((9 * gw, mid)),
             wide_eights,
             eights,
@@ -1499,7 +1563,7 @@
         [pltpu.VMEM((px, px), BF16)],
         flops=2 * n * px * cin * px,
         moved=n * px * cin * 4 + (mid + cin) * wide * 6 + cin * mid * 6,
-    )(planes, all_last, all_side, all_first, all_mid, wide_grads, mid_grads, first_grads)
+    )(planes, all_last, all_side, all_near, all_far, all_mid, wide_grads, mid_grads, first_grads)
 
     return (
         output.reshape(n, rows_out, cols_out, wide),

time: 344 us -> 337 us (0.980)
  Pallas kernels: 335 us -> 327 us
    pallas_call x2, Pallas kernels: 92.4 us -> 86.4 us  [the longest x1 53.4 us: per_device(): call(carrying(functools.partial(image_back_body, few, px, q), (7, 5, 1, 5...]
  transfers between devices with their start and end apart: 1 -> 1, of which waited for: 0 -> 0; matrix products, arithmetic and copies ran while one was open for 0% -> 0% of each run, Pallas kernels for 12% -> 11%
where the time goes in v1:
time: 337 us; the launch traced here: 336 us
  Pallas kernels  327 us (97%)
  starting transfers between devices  5.03 us (1%)
    pallas_call x1, Pallas kernels, per_device(): call(carrying(functools.partial(image_back_body, few, px, q), (7, 5, 1, 5...  53.4 us
    pallas_call x1, Pallas kernels, per_device(): call(carrying(functools.partial(conv_back_body, per, px, q, functools.par...  46.4 us
    pallas_call x1, Pallas kernels, per_device(): call(functools.partial(first_body, per, px, q, functools.partial(first_to...  37.6 us
    pallas_call x1, Pallas kernels, per_device(): call(functools.partial(last_grad_body, functools.partial(out_totals, cell...  36.9 us
    pallas_call x1, Pallas kernels, per_device(): call(carrying(functools.partial(mid_back_body, per, q, functools.partial(...  33.3 us
    pallas_call x1, Pallas kernels, per_device(): call(carrying(first_back_body, (5, 2, 2, 3, 1), carry_first), 'first_grad...  33 us
    pallas_call x1, Pallas kernels, per_device(): call(functools.partial(conv_body, per, px, q, functools.partial(mid_total...  29.3 us
    pallas_call x1, Pallas kernels, per_device(): call(functools.partial(place_body, px), 'image_places', (cuts,), [rows_sp...  20.8 us
  transfers between devices with their start and end apart: 1, of which 0 were waited for; matrix products, arithmetic and copies ran while one was open for 0% of the time, Pallas kernels for 11%

profile of v1, /device:TPU:0, one launch (start us, length us, event | category | flops | bytes accessed | tf_op | source)
XLA Modules:
  0.0 336.0 jit_solution(13895661224046423164)
XLA Ops:
  0.6 1.6 slice_bitcast_fusion
  2.3 5.0 %collective-permute-start = (bf16[24,32,1024]{2,1,0:T(8,128)(2,1)S(1)}, bf16[24,32,1024]{2,1,0:T(8,128)(2,1)S(1)}, u32[]{:S(2)}, u32[]{:S(2)}) collective-permute-start(bf16[24,32,1024]{2,1,0:T(8,128)(2,1)S(1)} %slice_bitcast_fusion), channel_id=1, source_target_pairs={{0,1},{1,2},{2,3},{4,5},{5,6},{6,7},{8,9},{9,10},{10,11},{12,13},{... | collective-permute-start | bytes 4718600 | tf_op jit(solution)/shard_map/ppermute | solution.py:1199
  7.3 37.6 %first_product.1 = (bf16[6144,1024]{1,0:T(8,128)(2,1)}, f32[6144,1024]{1,0:T(8,128)}, f32[1536,2048]{1,0:T(8,128)}, f32[8,1024]{1,0:T(8,128)}, f32[32,128]{1,0:T(8,128)}) custom-call(bf16[24,8,32,1024]{3,2,1,0:T(8,128)(2,1)} %img.1, bf16[1024,1024]{1,0:T(8,128)(2,1)} %refs_4_.1, bf16[1024,2048]{1,0:T(8,128)(2,1)} %refs_6_.1, f32[1024]{0:T(1024)} %gain.2, ...), custom_call_target="tpu_custom_call" | custom-call | flops 22548578304 | bytes 69206016 | tf_op jit(solution)/shard_map/first_product/pallas_call | solution.py:1216
  44.9 0.0 collective-permute-done.halo
  44.9 0.0 copy-start
  44.9 1.1 copy-done
  46.0 29.3 %grouped_conv.1 = (f32[1536,1024]{1,0:T(8,128)}, f32[8,1024]{1,0:T(8,128)}, f32[8,2048]{1,0:T(8,128)}) custom-call(f32[24,4,64,1024]{3,2,1,0:T(8,128)} %bitcast.12, bf16[24,32,1024]{2,1,0:T(8,128)(2,1)} %copy-done, bf16[1024,1024]{1,0:T(8,128)(2,1)} %refs_4_.1, f32[8,1024]{1,0:T(8,128)} %get-tuple-element.69.coef.refs_7_.refs_2_, ...), custom_call_target="tpu_custom_call" | custom-call | flops 8858370048 | bytes 31457280 | tf_op jit(solution)/shard_map/grouped_conv/pallas_call | solution.py:1253
  75.4 20.5 %last_product.1 = (bf16[1536,1024]{1,0:T(8,128)(2,1)}, f32[1536,2048]{1,0:T(8,128)}, f32[8,2048]{1,0:T(8,128)}, bf16[24,16,1024]{2,1,0:T(8,128)(2,1)}) custom-call(f32[1536,1024]{1,0:T(8,128)} %get-tuple-element.71.mid.refs_2_.refs_1_, f32[8,1024]{1,0:T(8,128)} %get-tuple-element.72.coef.refs_3_.refs_5_, bf16[1024,2048]{1,0:T(8,128)(2,1)} %refs_1_.1, ...), custom_call_target="tpu_custom_call" | custom-call | flops 6442450944 | bytes 22020096 | tf_op jit(solution)/shard_map/last_product/pallas_call | solution.py:1286
  95.8 16.1 %output.1 = (bf16[1536,2048]{1,0:T(8,128)(2,1)}, f32[48,128]{1,0:T(8,128)}) custom-call(f32[1536,2048]{1,0:T(8,128)} %get-tuple-element.74.last, f32[1536,2048]{1,0:T(8,128)} %get-tuple-element.75.side, bf16[1536,2048]{1,0:T(8,128)(2,1)} %bitcast.14, f32[8,2048]{1,0:T(8,128)} %get-tuple-element.76.coef), custom_call_target="tpu_custom_call" | custom-call | flops 94371840 | bytes 37748736 | tf_op jit(solution)/shard_map/output/pallas_call | solution.py:1301
  111.9 36.9 %last_gradients.1 = (bf16[1536,2048]{1,0:T(8,128)(2,1)}, bf16[1536,2048]{1,0:T(8,128)(2,1)}, bf16[1024,2048]{1,0:T(8,128)(2,1)}, f32[8,2048]{1,0:T(8,128)}, bf16[24,16,1024]{2,1,0:T(8,128)(2,1)}) custom-call(f32[1536,2048]{1,0:T(8,128)} %get-tuple-element.74.last, f32[1536,2048]{1,0:T(8,128)} %get-tuple-element.75.side, bf16[1536,2048]{1,0:T(8,128)(2,1)} %bitcast.15, ...), custom_call_target="tpu_custom_call" | custom-call | flops 6442450944 | bytes 51380224 | tf_op jit(solution)/shard_map/last_gradients/pallas_call | solution.py:1320
  148.8 33.3 %mid_back.1 = (f32[1536,1024]{1,0:T(8,128)}, f32[8,1024]{1,0:T(8,128)}, f32[8,1024]{1,0:T(8,128)}, bf16[24,16,1024]{2,1,0:T(8,128)(2,1)}, bf16[1024,2048]{1,0:T(8,128)(2,1)}, /*index=5*/bf16[512,2048]{1,0:T(8,128)(2,1)}) custom-call(bf16[1536,2048]{1,0:T(8,128)(2,1)} %get-tuple-element.81.refs_0_, bf16[1024,2048]{1,0:T(8,128)(2,1)} %refs_1_.1, ...), custom_call_target="tpu_custom_call" | custom-call | flops 12884901888 | bytes 36700160 | tf_op jit(solution)/shard_map/mid_back/pallas_call | solution.py:1349
  182.2 46.4 %grouped_conv_back.1 = (bf16[24,4,64,1024]{3,2,1,0:T(8,128)(2,1)}, bf16[9,32,1024]{2,1,0:T(8,128)(2,1)}, f32[8,1024]{1,0:T(8,128)}, f32[8,1024]{1,0:T(8,128)}, b...) custom-call(f32[1536,1024]{1,0:T(8,128)} %get-tuple-element.85.refs_0_, ...), custom_call_target="tpu_custom_call" | custom-call | flops 14495514624 | bytes 50331648 | tf_op jit(solution)/shard_map/grouped_conv_back/pallas_call | solution.py:1384
  228.6 33.0 %first_gradient.1 = (bf16[1024,512]{1,0:T(8,128)(2,1)}, bf16[1024,512]{1,0:T(8,128)(2,1)}, bf16[512,2048]{1,0:T(8,128)(2,1)}, bf16[512,2048]{1,0:T(8,128)(2,1)}, bf16[512,512]{1,0:T(8,128)(2,1)}) custom-call(bf16[6144,1024]{1,0:T(8,128)(2,1)} %bitcast.17, f32[6144,1024]{1,0:T(8,128)} %get-tuple-element.68.refs_1_, ...), custom_call_target="tpu_custom_call" | custom-call | flops 12884901888 | bytes 62914560 | tf_op jit(solution)/shard_map/first_gradient/pallas_call | solution.py:1453
  261.6 53.4 %image_gradient.1 = (bf16[6144,1024]{1,0:T(8,128)(2,1)}, bf16[1024,2048]{1,0:T(8,128)(2,1)}, bf16[1024,2048]{1,0:T(8,128)(2,1)}, bf16[1024,512]{1,0:T(8,128)(2,1...) custom-call(bf16[6144,1024]{1,0:T(8,128)(2,1)} %bitcast.18, f32[6144,1024]{1,0:T(8,128)} %get-tuple-element.68.refs_1_, ...), custom_call_target="tpu_custom_call" | custom-call | flops 19327352832 | bytes 56623104 | tf_op jit(solution)/shard_map/image_gradient/pallas_call | solution.py:1480
  315.1 20.8 %image_places.1 = (bf16[24,8,32,1024]{3,2,1,0:T(8,128)(2,1)}, f32[1024,2048]{1,0:T(8,128)}, f32[1024,2048]{1,0:T(8,128)}, f32[1024,1024]{1,0:T(8,128)}, f32[288,...) custom-call(bf16[6144,1024]{1,0:T(8,128)(2,1)} %get-tuple-element.10, ...), custom_call_target="tpu_custom_call" | custom-call | flops 3221225472 | bytes 56623104 | tf_op jit(solution)/shard_map/image_places/pallas_call | solution.py:1532
Async XLA Ops:
  2.3 42.6 %collective-permute-start = (bf16[24,32,1024]{2,1,0:T(8,128)(2,1)S(1)}, bf16[24,32,1024]{2,1,0:T(8,128)(2,1)S(1)}, u32[]{:S(2)}, u32[]{:S(2)}) collective-permute-start(bf16[24,32,1024]{2,1,0:T(8,128)(2,1)S(1)} %slice_bitcast_fusion), channel_id=1, source_target_pairs={{0,1},{1,2},{2,3},{4,5},{5,6},{6,7},{8,9},{9,10},{10,11},{12,13},{... | collective-permute-start | bytes 4718600 | tf_op jit(solution)/shard_map/ppermute | solution.py:1199
  44.9 1.1 copy-start

commit v2 on v1

--- a/solution.py
+++ b/solution.py
@@ -1284,11 +1284,11 @@
     rim_spec = pl.BlockSpec((per, cols_out, mid), lambda s: (s, 0, 0))
     rim_shape = shape((n, cols_out, mid), BF16)
     mid_act, last_pre, coef3, rim_own = call(
-        functools.partial(last_body, per, q, functools.partial(last_totals, cells_out, wide)),
+        functools.partial(last_body, 2 * per, q, functools.partial(last_totals, cells_out, wide)),
         "last_product",
-        (steps,),
-        [rows_spec(rows, mid), eights, whole((mid, wide))] + [whole((wide,))] * 4 + [wide_eights],
-        [rows_spec(rows, mid), rows_spec(rows, wide), wide_eights, rim_spec],
+        (steps // 2,),
+        [rows_spec(2 * rows, mid), eights, whole((mid, wide))] + [whole((wide,))] * 4 + [wide_eights],
+        [rows_spec(2 * rows, mid), rows_spec(2 * rows, wide), wide_eights, pl.BlockSpec((2 * per, cols_out, mid), lambda s: (s, 0, 0))],
         [shape((n * q, mid), BF16), shape((n * q, wide)), shape((8, wide)), rim_shape],
         [pltpu.VMEM((16, wide), F32)] + exchange_scratch(2 * wide // LANES),
         flops=2 * n * q * mid * wide,

time: 337 us -> 336 us (level)
  no operation moved by 1% of the time
where the time goes in v2:
time: 336 us; the launch traced here: 335 us
  Pallas kernels  327 us (97%)
  starting transfers between devices  5.03 us (1%)
    pallas_call x1, Pallas kernels, per_device(): call(carrying(functools.partial(image_back_body, few, px, q), (7, 5, 1, 5...  53.4 us
    pallas_call x1, Pallas kernels, per_device(): call(carrying(functools.partial(conv_back_body, per, px, q, functools.par...  46.4 us
    pallas_call x1, Pallas kernels, per_device(): call(functools.partial(first_body, per, px, q, functools.partial(first_to...  37.6 us
    pallas_call x1, Pallas kernels, per_device(): call(functools.partial(last_grad_body, functools.partial(out_totals, cell...  36.9 us
    pallas_call x1, Pallas kernels, per_device(): call(carrying(functools.partial(mid_back_body, per, q, functools.partial(...  33.3 us
    pallas_call x1, Pallas kernels, per_device(): call(carrying(first_back_body, (5, 2, 2, 3, 1), carry_first), 'first_grad...  33 us
    pallas_call x1, Pallas kernels, per_device(): call(functools.partial(conv_body, per, px, q, functools.partial(mid_total...  29.3 us
    pallas_call x1, Pallas kernels, per_device(): call(functools.partial(place_body, px), 'image_places', (cuts,), [rows_sp...  20.8 us
  transfers between devices with their start and end apart: 1, of which 0 were waited for; matrix products, arithmetic and copies ran while one was open for 0% of the time, Pallas kernels for 11%

profile of v2, /device:TPU:0, one launch (start us, length us, event | category | flops | bytes accessed | tf_op | source)
XLA Modules:
  0.0 335.5 jit_solution(7558324542683099007)
XLA Ops:
  0.6 1.6 slice_bitcast_fusion
  2.3 5.0 %collective-permute-start = (bf16[24,32,1024]{2,1,0:T(8,128)(2,1)S(1)}, bf16[24,32,1024]{2,1,0:T(8,128)(2,1)S(1)}, u32[]{:S(2)}, u32[]{:S(2)}) collective-permute-start(bf16[24,32,1024]{2,1,0:T(8,128)(2,1)S(1)} %slice_bitcast_fusion), channel_id=1, source_target_pairs={{0,1},{1,2},{2,3},{4,5},{5,6},{6,7},{8,9},{9,10},{10,11},{12,13},{... | collective-permute-start | bytes 4718600 | tf_op jit(solution)/shard_map/ppermute | solution.py:1199
  7.3 37.6 %first_product.1 = (bf16[6144,1024]{1,0:T(8,128)(2,1)}, f32[6144,1024]{1,0:T(8,128)}, f32[1536,2048]{1,0:T(8,128)}, f32[8,1024]{1,0:T(8,128)}, f32[32,128]{1,0:T(8,128)}) custom-call(bf16[24,8,32,1024]{3,2,1,0:T(8,128)(2,1)} %img.1, bf16[1024,1024]{1,0:T(8,128)(2,1)} %refs_4_.1, bf16[1024,2048]{1,0:T(8,128)(2,1)} %refs_6_.1, f32[1024]{0:T(1024)} %gain.2, ...), custom_call_target="tpu_custom_call" | custom-call | flops 22548578304 | bytes 69206016 | tf_op jit(solution)/shard_map/first_product/pallas_call | solution.py:1216
  44.9 0.0 collective-permute-done.halo
  44.9 0.0 copy-start
  44.9 1.1 copy-done
  46.0 29.3 %grouped_conv.1 = (f32[1536,1024]{1,0:T(8,128)}, f32[8,1024]{1,0:T(8,128)}, f32[8,2048]{1,0:T(8,128)}) custom-call(f32[24,4,64,1024]{3,2,1,0:T(8,128)} %bitcast.12, bf16[24,32,1024]{2,1,0:T(8,128)(2,1)} %copy-done, bf16[1024,1024]{1,0:T(8,128)(2,1)} %refs_4_.1, f32[8,1024]{1,0:T(8,128)} %get-tuple-element.69.coef.refs_7_.refs_2_, ...), custom_call_target="tpu_custom_call" | custom-call | flops 8858370048 | bytes 31457280 | tf_op jit(solution)/shard_map/grouped_conv/pallas_call | solution.py:1253
  75.4 20.0 %last_product.1 = (bf16[1536,1024]{1,0:T(8,128)(2,1)}, f32[1536,2048]{1,0:T(8,128)}, f32[8,2048]{1,0:T(8,128)}, bf16[24,16,1024]{2,1,0:T(8,128)(2,1)}) custom-call(f32[1536,1024]{1,0:T(8,128)} %get-tuple-element.71.mid.refs_2_.refs_1_, f32[8,1024]{1,0:T(8,128)} %get-tuple-element.72.coef.refs_3_.refs_5_, bf16[1024,2048]{1,0:T(8,128)(2,1)} %refs_1_.1, ...), custom_call_target="tpu_custom_call" | custom-call | flops 6442450944 | bytes 22020096 | tf_op jit(solution)/shard_map/last_product/pallas_call | solution.py:1286
  95.3 16.1 %output.1 = (bf16[1536,2048]{1,0:T(8,128)(2,1)}, f32[48,128]{1,0:T(8,128)}) custom-call(f32[1536,2048]{1,0:T(8,128)} %get-tuple-element.74.last, f32[1536,2048]{1,0:T(8,128)} %get-tuple-element.75.side, bf16[1536,2048]{1,0:T(8,128)(2,1)} %bitcast.14, f32[8,2048]{1,0:T(8,128)} %get-tuple-element.76.coef), custom_call_target="tpu_custom_call" | custom-call | flops 94371840 | bytes 37748736 | tf_op jit(solution)/shard_map/output/pallas_call | solution.py:1301
  111.4 36.9 %last_gradients.1 = (bf16[1536,2048]{1,0:T(8,128)(2,1)}, bf16[1536,2048]{1,0:T(8,128)(2,1)}, bf16[1024,2048]{1,0:T(8,128)(2,1)}, f32[8,2048]{1,0:T(8,128)}, bf16[24,16,1024]{2,1,0:T(8,128)(2,1)}) custom-call(f32[1536,2048]{1,0:T(8,128)} %get-tuple-element.74.last, f32[1536,2048]{1,0:T(8,128)} %get-tuple-element.75.side, bf16[1536,2048]{1,0:T(8,128)(2,1)} %bitcast.15, ...), custom_call_target="tpu_custom_call" | custom-call | flops 6442450944 | bytes 51380224 | tf_op jit(solution)/shard_map/last_gradients/pallas_call | solution.py:1320
  148.3 33.3 %mid_back.1 = (f32[1536,1024]{1,0:T(8,128)}, f32[8,1024]{1,0:T(8,128)}, f32[8,1024]{1,0:T(8,128)}, bf16[24,16,1024]{2,1,0:T(8,128)(2,1)}, bf16[1024,2048]{1,0:T(8,128)(2,1)}, /*index=5*/bf16[512,2048]{1,0:T(8,128)(2,1)}) custom-call(bf16[1536,2048]{1,0:T(8,128)(2,1)} %get-tuple-element.81.refs_0_, bf16[1024,2048]{1,0:T(8,128)(2,1)} %refs_1_.1, ...), custom_call_target="tpu_custom_call" | custom-call | flops 12884901888 | bytes 36700160 | tf_op jit(solution)/shard_map/mid_back/pallas_call | solution.py:1349
  181.7 46.4 %grouped_conv_back.1 = (bf16[24,4,64,1024]{3,2,1,0:T(8,128)(2,1)}, bf16[9,32,1024]{2,1,0:T(8,128)(2,1)}, f32[8,1024]{1,0:T(8,128)}, f32[8,1024]{1,0:T(8,128)}, b...) custom-call(f32[1536,1024]{1,0:T(8,128)} %get-tuple-element.85.refs_0_, ...), custom_call_target="tpu_custom_call" | custom-call | flops 14495514624 | bytes 50331648 | tf_op jit(solution)/shard_map/grouped_conv_back/pallas_call | solution.py:1384
  228.1 33.0 %first_gradient.1 = (bf16[1024,512]{1,0:T(8,128)(2,1)}, bf16[1024,512]{1,0:T(8,128)(2,1)}, bf16[512,2048]{1,0:T(8,128)(2,1)}, bf16[512,2048]{1,0:T(8,128)(2,1)}, bf16[512,512]{1,0:T(8,128)(2,1)}) custom-call(bf16[6144,1024]{1,0:T(8,128)(2,1)} %bitcast.17, f32[6144,1024]{1,0:T(8,128)} %get-tuple-element.68.refs_1_, ...), custom_call_target="tpu_custom_call" | custom-call | flops 12884901888 | bytes 62914560 | tf_op jit(solution)/shard_map/first_gradient/pallas_call | solution.py:1453
  261.1 53.4 %image_gradient.1 = (bf16[6144,1024]{1,0:T(8,128)(2,1)}, bf16[1024,2048]{1,0:T(8,128)(2,1)}, bf16[1024,2048]{1,0:T(8,128)(2,1)}, bf16[1024,512]{1,0:T(8,128)(2,1...) custom-call(bf16[6144,1024]{1,0:T(8,128)(2,1)} %bitcast.18, f32[6144,1024]{1,0:T(8,128)} %get-tuple-element.68.refs_1_, ...), custom_call_target="tpu_custom_call" | custom-call | flops 19327352832 | bytes 56623104 | tf_op jit(solution)/shard_map/image_gradient/pallas_call | solution.py:1480
  314.5 20.8 %image_places.1 = (bf16[24,8,32,1024]{3,2,1,0:T(8,128)(2,1)}, f32[1024,2048]{1,0:T(8,128)}, f32[1024,2048]{1,0:T(8,128)}, f32[1024,1024]{1,0:T(8,128)}, f32[288,...) custom-call(bf16[6144,1024]{1,0:T(8,128)(2,1)} %get-tuple-element.10, ...), custom_call_target="tpu_custom_call" | custom-call | flops 3221225472 | bytes 56623104 | tf_op jit(solution)/shard_map/image_places/pallas_call | solution.py:1532
Async XLA Ops:
  2.3 42.6 %collective-permute-start = (bf16[24,32,1024]{2,1,0:T(8,128)(2,1)S(1)}, bf16[24,32,1024]{2,1,0:T(8,128)(2,1)S(1)}, u32[]{:S(2)}, u32[]{:S(2)}) collective-permute-start(bf16[24,32,1024]{2,1,0:T(8,128)(2,1)S(1)} %slice_bitcast_fusion), channel_id=1, source_target_pairs={{0,1},{1,2},{2,3},{4,5},{5,6},{6,7},{8,9},{9,10},{10,11},{12,13},{... | collective-permute-start | bytes 4718600 | tf_op jit(solution)/shard_map/ppermute | solution.py:1199
  44.9 1.1 copy-start
